TPU v7x, 128 devices: a whole 4x4x4 slice. The times are simulated.
128 devices in a mesh: grp: 4 (over z_lo, core), cp: 32 (over x, y, z_hi).
Axes of the slice: x: 4, y: 4, z: 4 (z_hi: 2, z_lo: 2; z = z_hi * 2 + z_lo), core: 2. Of those that a mesh axis runs over, the one named last changes fastest.
Arguments:
- queries: bfloat16 [3, 32, 73728], P(None, 'cp'), may hold values from -25 to 25, as said below
- cache: bfloat16 [3, 65536, 576], P(None, 'cp'), may hold values from -5 to 5
- value_up_weight: bfloat16 [128, 512, 128], P('cp'), may hold values from -0.25 to 0.25
- w_out: bfloat16 [16384, 7168], P('cp'), may hold values from -0.375 to 0.375
- resid: bfloat16 [3, 32, 7168], P(None, 'cp'), may hold values from -1.5 to 1.5
- norm_gain: float32 [7168], replicated, may hold values from 0.5 to 1.5
- routes: int32 [3, 32, 4], P(None, 'cp'), may hold values from 0 to 7, all different within a row
- route_weight: bfloat16 [3, 32, 4], P(None, 'cp'), may hold values from 0.099609375 to 1
- w_gate: bfloat16 [32, 7168, 512], P('cp', 'grp'), may hold values from -0.0625 to 0.0625
- w_up: bfloat16 [32, 7168, 512], P('cp', 'grp'), may hold values from -0.0625 to 0.0625
- w_down: bfloat16 [32, 512, 7168], P('cp', None, 'grp'), may hold values from -0.125 to 0.125
Outputs:
- mixed: bfloat16 [3, 32, 7168], P(None, 'cp')
Inputs may be any that keep to these rules, and one draw needn't show every extreme that they name: `queries`: query entries.
All inputs are finite; a program needn't handle non-finite values.
Results may differ from a plain program's by a relative error of at most 0.014.
Values may be sent and summed in bfloat16 or wider, within the bound.
A program may use at most 192 MiB of HBM per device.

v0:
```python
import jax
import jax.numpy as jnp
from jax import lax
from jax.sharding import PartitionSpec as P

D = 7168
H = 128
KVL = 512
DV = 128
SPLIT = 4
QROWS = 32
CTX_DEV = 2048
QK = 576


score_scale = 192.0 ** (-0.5)


def attend_latent(query_rows, key_rows, offset, total_len):
    query_block = query_rows.reshape(query_rows.shape[0], H, QK)
    scores = (
        jnp.einsum("qhk,tk->qht", query_block, key_rows, preferred_element_type=jnp.float32)
        * score_scale
    )
    position_list = offset + jnp.arange(key_rows.shape[0], dtype=jnp.int32)
    query_pos = total_len - query_block.shape[0] + jnp.arange(query_block.shape[0], dtype=jnp.int32)
    allowed = position_list[None, None, :] <= query_pos[:, None, None]
    scores = jnp.where(allowed, scores, -1e30)
    row_peak = jnp.max(scores, axis=-1)
    weights_exp = jnp.where(allowed, jnp.exp(scores - row_peak[..., None]), 0.0)
    row_total = jnp.sum(weights_exp, axis=-1)
    row_output = jnp.einsum(
        "qht,tv->qhv",
        weights_exp.astype(jnp.bfloat16),
        key_rows[:, :KVL],
        preferred_element_type=jnp.float32,
    )
    return (row_peak, row_total, row_output / row_total[..., None])


def on_device(
    queries,
    cache,
    value_up_weight,
    w_out,
    resid,
    norm_gain,
    routes,
    route_weight,
    w_gate,
    w_up,
    w_down,
):
    group = lax.axis_index("grp")
    column = lax.axis_index("cp")
    cp_count = lax.axis_size("cp")
    grp_count = lax.axis_size("grp")
    seqs = queries.shape[0]
    sequence = jnp.minimum(group, seqs - 1)
    active = group < seqs
    own_queries = lax.dynamic_index_in_dim(queries, sequence, 0, keepdims=False)
    all_queries = lax.all_gather(own_queries, "cp", axis=0, tiled=True)
    key_rows = lax.dynamic_index_in_dim(cache, sequence, 0, keepdims=False)
    offset = column * CTX_DEV
    total_len = CTX_DEV * cp_count

    def run_block(operand):
        return attend_latent(operand, key_rows, offset, total_len)

    def skip_block(operand):
        return (
            jnp.zeros((QROWS, H), jnp.float32),
            jnp.ones((QROWS, H), jnp.float32),
            jnp.zeros((QROWS, H, KVL), jnp.float32),
        )

    row_peak, row_total, row_output = lax.cond(active, run_block, skip_block, all_queries)
    heads_here = value_up_weight.shape[0]
    piece_list = (
        lax.all_to_all(row_peak[None], "cp", split_axis=2, concat_axis=0, tiled=True),
        lax.all_to_all(row_total[None], "cp", split_axis=2, concat_axis=0, tiled=True),
        lax.all_to_all(row_output[None], "cp", split_axis=2, concat_axis=0, tiled=True),
    )
    peak_overall = jnp.max(piece_list[0], axis=0)
    block_weight = piece_list[1] * jnp.exp(piece_list[0] - peak_overall[None])
    own_heads = (
        jnp.sum(block_weight[..., None] * piece_list[2], axis=0)
        / jnp.sum(block_weight, axis=0)[..., None]
    )
    latent_state = own_heads.astype(jnp.bfloat16)
    head_list = jnp.einsum(
        "mtz,tzu->mtu", latent_state, value_up_weight, preferred_element_type=jnp.float32
    ).astype(jnp.bfloat16)
    head_list = head_list.reshape(QROWS, heads_here * DV)
    partial_rows = jnp.dot(head_list, w_out, preferred_element_type=jnp.float32)
    attn_rows = lax.psum_scatter(partial_rows, "cp", scatter_dimension=0, tiled=True)
    own_resid = lax.dynamic_index_in_dim(resid, sequence, 0, keepdims=False)
    hidden = (own_resid.astype(jnp.float32) + attn_rows).astype(jnp.bfloat16)
    hidden_f = hidden.astype(jnp.float32)
    normed = (
        hidden_f
        * lax.rsqrt(jnp.mean(hidden_f * hidden_f, axis=-1, keepdims=True) + 1e-06)
        * norm_gain
    ).astype(jnp.bfloat16)
    own_routes = lax.dynamic_index_in_dim(routes, sequence, 0, keepdims=False)
    own_weight = lax.dynamic_index_in_dim(route_weight, sequence, 0, keepdims=False)
    expert_of = jnp.arange(cp_count, dtype=jnp.int32) // SPLIT
    matches = own_routes[None, :, :] == expert_of[:, None, None]
    present = jnp.any(matches, axis=-1)
    slot_weight = jnp.sum(
        jnp.where(matches, own_weight.astype(jnp.float32)[None], 0.0), axis=-1
    ).astype(jnp.bfloat16)
    outgoing = jnp.where(present[..., None], normed[None], jnp.zeros((), jnp.bfloat16))
    arrived, arrived_weight = (
        lax.all_to_all(outgoing, "cp", split_axis=0, concat_axis=0, tiled=True),
        lax.all_to_all(slot_weight, "cp", split_axis=0, concat_axis=0, tiled=True),
    )
    slots, slot_wts, column_hidden = (
        lax.all_gather(arrived, "grp", axis=0, tiled=True),
        lax.all_gather(arrived_weight, "grp", axis=0, tiled=True),
        lax.all_gather(hidden, "grp", axis=0, tiled=True),
    )
    rows_here = hidden.shape[0]
    slots = slots[: seqs * cp_count]
    slot_wts = slot_wts[: seqs * cp_count].astype(jnp.float32).reshape(-1)
    column_hidden = column_hidden[: seqs * rows_here].reshape(seqs, rows_here, D)
    rows_in = slots.reshape(seqs * cp_count * rows_here, D)
    quarter = D // grp_count
    own_columns = lax.dynamic_slice_in_dim(rows_in, group * quarter, quarter, 1)
    gate_sums = jnp.dot(own_columns, w_gate[0], preferred_element_type=jnp.float32)
    up_sums = jnp.dot(own_columns, w_up[0], preferred_element_type=jnp.float32)
    gate_sums, up_sums = lax.psum((gate_sums, up_sums), "grp")
    units = (jax.nn.silu(gate_sums) * up_sums).astype(jnp.bfloat16)
    part = jnp.dot(units, w_down[0], preferred_element_type=jnp.float32).astype(jnp.bfloat16)
    weighted = (part.astype(jnp.float32) * slot_wts[:, None]).reshape(
        seqs, cp_count, rows_here, quarter
    )
    summed = lax.psum_scatter(weighted, "cp", scatter_dimension=1, tiled=True)
    resid_part = lax.dynamic_slice_in_dim(column_hidden, group * quarter, quarter, 2)
    mixed_part = (resid_part.astype(jnp.float32) + summed[:, 0]).astype(jnp.bfloat16)
    mixed = lax.all_gather(mixed_part, "grp", axis=2, tiled=True)
    return mixed


def solution(mesh):
    placed = (
        P(None, "cp", None),
        P(None, "cp", None),
        P("cp", None, None),
        P("cp", None),
        P(None, "cp", None),
        P(),
        P(None, "cp", None),
        P(None, "cp", None),
        P("cp", "grp", None),
        P("cp", "grp", None),
        P("cp", None, "grp"),
    )
    return jax.shard_map(
        on_device, mesh=mesh, in_specs=placed, out_specs=P(None, "cp", None), check_vma=False
    )
```

profile of v0, /device:TPU:1, one launch (start us, length us, event | category | flops | bytes accessed | tf_op | source)
XLA Modules:
  0.0 1221.1 jit_solution(13247553261257040495)
XLA Ops:
  6.5 2.2 dynamic-slice_bitcast_fusion.1
  8.8 115.5 %all-gather.9.cloned.1.call-done = bf16[32,1,73728]{2,1,0:T(2,128)(2,1)} async-done(((bf16[1,1,73728]{2,1,0:T(2,128)(2,1)}), bf16[32,1,73728]{2,1,0:T(2,128)(2,1)}) %all-gather.9.cloned.1.call-update) | async-done | bytes 4718608 | tf_op jit(solution)/shard_map/all_gather | solution.py:62
  124.2 100.2 %conditional.1 = (f32[32,128]{1,0:T(8,128)}, f32[32,128]{1,0:T(8,128)}, f32[32,128,512]{2,1,0:T(8,128)}) conditional(s32[]{:T(128)} %convert_element_type.83, () %tuple.18, (s32[]{:T(128)}, bf16[3,2048,576]{1,2,0:T(8,128)(2,1)}, s32[]{:T(128)}, bf16[32,1,73728]{2,1,0:T(2,128)(2,1)}) %tuple.19), branch_computations={%region_0.1_spmd, %region_1.4_spmd} | conditional | flops 18364819456 | bytes 276923200 | solution.py:77
  124.3 0.1 broadcast_compare_fusion
  124.4 29.2 %reduce.4 = bf16[32,73728]{1,0:T(8,128)(2,1)} reduce(bf16[32,1,73728]{2,1,0:T(2,128)(2,1)} %get-tuple-element.48, bf16[]{:T(256)} %constant.130), dimensions={1}, to_apply=%get-tuple-element.48.reduce_sub_computation | reduce | bytes 9437186 | tf_op jit(solution)/shard_map/cond
  153.6 8.8 reshape.315
  162.4 22.7 %fusion = (f32[32,128]{1,0:T(8,128)}, f32[2048,32,128]{2,0,1:T(8,128)S(1)}) fusion(pred[32,2048]{1,0:T(8,128)(4,1)S(1)} %broadcast_compare_fusion, bf16[32,128,576]{2,1,0:T(8,128)(2,1)} %reshape.315, bf16[3,2048,576]{1,2,0:T(8,128)(2,1)} %get-tuple-element.47, s32[]{:T(128)} %get-tuple-element.38), kind=kOutput, calls=%fused_computation.2 | convolution fusion | flops 9688838144 | bytes 41239040 | tf_op jit(solution)/shard_map/cond/branch_1_fun/qhk,tk->qht/dot_general | solution.py:22
  185.1 13.5 %fusion.2 = f32[32,128]{1,0:T(8,128)} fusion(f32[2048,32,128]{2,0,1:T(8,128)S(1)} %get-tuple-element.56, f32[32,128]{1,0:T(8,128)} %get-tuple-element.60, pred[32,2048]{1,0:T(8,128)(4,1)S(1)} %broadcast_compare_fusion), kind=kLoop, calls=%fused_computation.4 | loop fusion | flops 41938944 | bytes 33652736 | tf_op jit(solution)/shard_map/cond/branch_1_fun/reduce_sum | solution.py:31
  198.6 1.9 dynamic-slice_bitcast_fusion
  200.6 23.9 %broadcast_divide_fusion = f32[32,128,512]{2,1,0:T(8,128)} fusion(f32[32,128]{1,0:T(8,128)} %fusion.2, bf16[2048,576]{0,1:T(8,128)(2,1)S(1)} %dynamic-slice_bitcast_fusion, f32[2048,32,128]{2,0,1:T(8,128)} %copy-done.1, f32[32,128]{1,0:T(8,128)} %get-tuple-element.60, pred[32,2048]{1,0:T(8,128)(4,1)S(1)} %broadcast_compare_fusion), kind=kOutput, calls=%fused_computation.7 | convolution fusion | flops 8633974784 | bytes 44138496 | tf_op jit(solution)/shard_map/cond/branch_1_fun/qht,tv->qhv/dot_general | solution.py:32
  224.4 0.8 copy.73
  225.2 0.5 broadcast.239
  225.8 0.7 reduce.10
  226.5 0.7 reshape.353
  227.2 5.5 all-to-all-start.1
  232.6 0.8 copy.72
  233.5 0.7 reduce.8
  234.2 0.7 reshape.351
  234.9 6.2 all-to-all-done.1
  241.0 3.8 all-to-all-start
  244.9 11.5 copy.101
  256.3 9.4 all-to-all-start.2
  265.8 0.6 reduce.11
  266.4 0.1 reshape.354
  266.6 0.6 reduce.9
  267.2 0.1 reshape.352
  267.4 0.5 copy.74
  268.1 124.9 %all-to-all-done.2 = f32[1,32,128,512]{3,1,0,2:T(8,128)} async-done(((f32[1,32,128,512]{3,1,0,2:T(8,128)}), f32[1,32,128,512]{3,1,0,2:T(8,128)}, u32[]{:S(2)}, u32[]{:S(2)}) %all-to-all-start.2) | async-done | bytes 8388640 | tf_op jit(solution)/shard_map/all_to_all | solution.py:82
  393.0 10.5 fusion.13
  403.5 0.1 divide_convert_fusion
  403.6 0.2 fusion.21
  403.8 5.5 fusion.28
  409.3 0.3 all-gather.7.cloned.1.call-start
  409.6 0.7 dynamic-slice.7
  410.3 0.7 fusion.36
  411.0 330.9 %all-reduce.8.cloned.1.call-done = f32[32,7168]{1,0:T(8,128)} async-done(((f32[32,7168]{1,0:T(8,128)}), f32[32,7168]{1,0:T(8,128)}) %all-reduce.8.cloned.1.call-update) | async-done | bytes 917520
  741.9 2.3 multiply_reduce_fusion
  744.9 0.1 convert_reduce_fusion
  745.0 0.7 broadcast_select_fusion
  745.7 0.5 broadcast.243
  746.2 3.4 reduce.12
  749.6 0.3 reshape.355
  749.9 16.3 %all_to_all.68 = bf16[32,2,3584]{2,1,0:T(2,128)(2,1)S(1)} all-to-all(bf16[32,2,3584]{2,1,0:T(2,128)(2,1)S(1)} %reshape.355), channel_id=1, replica_groups=mesh['grp'=4,'cp'=32] {'cp'}, dimensions={0} | all-to-all | bytes 917504 | tf_op jit(solution)/shard_map/all_to_all | solution.py:115
  766.2 0.4 reshape.356
  766.5 0.9 copy.80
  767.5 44.3 %all-gather.7.cloned.1.call-done = bf16[128,1,7168]{2,0,1:T(8,128)(2,1)} async-done(((bf16[32,1,7168]{2,0,1:T(8,128)(2,1)}), bf16[128,1,7168]{2,0,1:T(8,128)(2,1)}) %all-gather.7.cloned.1.call-update) | async-done | bytes 1835024 | tf_op jit(solution)/shard_map/all_gather | solution.py:119
  811.9 1.4 slice.22
  813.3 2.6 fusion.19
  815.9 2.6 fusion.17
  818.7 0.7 copy.81
  819.4 9.1 all-to-all-start.4
  828.6 0.6 dynamic-slice.5
  829.8 7.2 all-to-all-done.4
  837.0 0.3 reduce.6
  837.3 0.2 dynamic-update-slice
  837.6 6.6 all-reduce
  844.1 12.8 %all-reduce.12.cloned.1.call-done = (f32[96,512]{1,0:T(8,128)}, f32[96,512]{1,0:T(8,128)}) async-done(((f32[96,512]{1,0:T(8,128)}, f32[96,512]{1,0:T(8,128)}), (f32[96,512]{1,0:T(8,128)}, f32[96,512]{1,0:T(8,128)})) %all-reduce.12.cloned.1.call-update) | async-done | bytes 393232 | tf_op jit(solution)/shard_map/psum | solution.py:132
  856.9 1.4 fusion.15
  858.4 1.6 copy.82
  859.9 5.4 all-gather.3
  865.5 319.4 %all-reduce.10.cloned.1.call-done = f32[3,32,1,1792]{3,2,0,1:T(1,128)} async-done(((f32[3,32,1,1792]{3,2,0,1:T(1,128)}), f32[3,32,1,1792]{3,2,0,1:T(1,128)}) %all-reduce.10.cloned.1.call-update) | async-done | bytes 688144
  1184.8 1.4 constant_dynamic-slice_fusion.2
  1186.3 27.7 %all-gather.2 = bf16[3,7168]{1,0:T(4,128)(2,1)S(1)} all-gather(bf16[3,1792]{1,0:T(4,128)(2,1)S(1)} %fusion.31), channel_id=4, replica_groups=mesh['grp'=4,'cp'=32] {'grp'}, dimensions={1}, use_global_device_ids=true | all-gather | bytes 53760 | tf_op jit(solution)/shard_map/all_gather | solution.py:141
  1213.9 0.6 copy.114
  (40 shorter events, 0.8 us)
Async XLA Ops:
  6.5 850.4 %copy-start = (bf16[1,512,1792]{2,1,0:T(8,128)(2,1)S(1)}, bf16[1,512,1792]{2,1,0:T(8,128)(2,1)}, u32[]{:S(2)}) copy-start(bf16[1,512,1792]{2,1,0:T(8,128)(2,1)} %param.23) | copy-start | bytes 5505028
  6.5 117.7 %all-gather.9.cloned.1.call-start = ((), (), s32[]{:S(2)}) async-start(), calls=%async_computation.6 | async-start | bytes 9732096 | tf_op jit(solution)/shard_map/all_gather | solution.py:62
  185.1 13.5 %copy-start.1 = (f32[2048,32,128]{2,0,1:T(8,128)}, f32[2048,32,128]{2,0,1:T(8,128)S(1)}, u32[]{:S(2)}) copy-start(f32[2048,32,128]{2,0,1:T(8,128)S(1)} %get-tuple-element.56) | copy-start | bytes 100663296 | tf_op jit(solution)/shard_map/cond
  227.2 13.9 %all-to-all-start.1 = ((f32[32,1,128]{2,1,0:T(1,128)}), f32[32,1,128]{2,1,0:T(1,128)S(1)}, u32[]{:S(2)}, u32[]{:S(2)}) async-start(f32[32,1,128]{2,1,0:T(1,128)} %reshape.353), calls=%async_computation.1 | async-start | bytes 32768 | tf_op jit(solution)/shard_map/all_to_all | solution.py:80
  241.0 15.3 %all-to-all-start = ((f32[32,1,128]{2,1,0:T(1,128)}), f32[32,1,128]{2,1,0:T(1,128)S(1)}, u32[]{:S(2)}, u32[]{:S(2)}) async-start(f32[32,1,128]{2,1,0:T(1,128)} %reshape.351), calls=%async_computation | async-start | bytes 32768 | tf_op jit(solution)/shard_map/all_to_all | solution.py:81
  256.3 136.6 %all-to-all-start.2 = ((f32[1,32,128,512]{3,1,0,2:T(8,128)}), f32[1,32,128,512]{3,1,0,2:T(8,128)}, u32[]{:S(2)}, u32[]{:S(2)}) async-start(f32[1,32,128,512]{3,1,0,2:T(8,128)} %bitcast.112), calls=%async_computation.2 | async-start | bytes 16777216 | tf_op jit(solution)/shard_map/all_to_all | solution.py:82
  265.7 137.9 %copy-start.2 = (bf16[4,512,128]{2,1,0:T(8,128)(2,1)S(1)}, bf16[4,512,128]{2,1,0:T(8,128)(2,1)}, u32[]{:S(2)}) copy-start(bf16[4,512,128]{2,1,0:T(8,128)(2,1)} %param.15) | copy-start | bytes 1572868
  265.7 476.2 %all-reduce.8.cloned.1.call-start = ((), (), s32[]{:S(2)}) async-start(), calls=%async_computation.7 | async-start | bytes 1835008
  403.5 6.1 copy-start.7
  403.5 338.4 %copy-start.4 = (bf16[3,1,7168]{2,0,1:T(4,128)(2,1)S(1)}, bf16[3,1,7168]{2,0,1:T(4,128)(2,1)}, u32[]{:S(2)}) copy-start(bf16[3,1,7168]{2,0,1:T(4,128)(2,1)} %param.17) | copy-start | bytes 129028
  403.5 341.4 %copy-start.3 = (f32[7168]{0:T(1024)S(1)}, f32[7168]{0:T(1024)}, u32[]{:S(2)}) copy-start(f32[7168]{0:T(1024)} %param.18) | copy-start | bytes 86020
  409.3 409.2 %copy-start.5 = (bf16[3,1,4]{2,0,1:T(4,128)(2,1)S(1)}, bf16[3,1,4]{2,0,1:T(4,128)(2,1)}, u32[]{:S(2)}) copy-start(bf16[3,1,4]{2,0,1:T(4,128)(2,1)} %param.20) | copy-start | bytes 76
  409.3 419.2 %copy-start.6 = (u32[128]{0:T(128)S(1)}, u32[128]{0:T(128)}, u32[]{:S(2)}) copy-start(u32[128]{0:T(128)} %constant.117) | copy-start | bytes 1540
  409.3 402.6 %all-gather.7.cloned.1.call-start = ((), (), s32[]{:S(2)}) async-start(), calls=%async_computation.5 | async-start | bytes 2293760 | tf_op jit(solution)/shard_map/all_gather | solution.py:119
  767.5 89.4 %all-reduce.12.cloned.1.call-start = ((), (), s32[]{:S(2)}) async-start(), calls=%async_computation.9 | async-start | bytes 786432 | tf_op jit(solution)/shard_map/psum | solution.py:132
  819.4 17.6 %all-to-all-start.4 = ((bf16[32,1,1]{2,1,0:T(2,128)(2,1)}), bf16[32,1,1]{2,1,0:T(2,128)(2,1)S(1)}, u32[]{:S(2)}, u32[]{:S(2)}) async-start(bf16[32,1,1]{2,1,0:T(2,128)(2,1)} %copy.81), calls=%async_computation.4 | async-start | bytes 32768 | tf_op jit(solution)/shard_map/all_to_all | solution.py:116
  828.5 356.3 %all-reduce.10.cloned.1.call-start = ((), (), s32[]{:S(2)}) async-start(), calls=%async_computation.8 | async-start | bytes 1376256
Sparse Core Ops, SparseCore 0:
  10.3 113.8 all-gather.8
  409.4 332.3 all-reduce.7
  767.6 44.2 all-gather.6
  818.7 38.1 all-reduce.11
  860.1 324.7 all-reduce.9
where the time goes:
time: 1220 us
  waiting for transfers between devices  961 us (79%)
  other arithmetic  63.2 us (5%)
  matrix products  58.9 us (5%)
  blocking collectives  55.9 us (5%)
  local copies, waits for them, and re-layouts  39 us (3%)
  starting transfers between devices  28.1 us (2%)
  between operations  14.8 us (1%)
    unnamed x7, waiting for transfers between devices  650 us
    all_to_all x1, waiting for transfers between devices, on_device(): lax.all_to_all(row_output[None], 'cp', split_axis=2, concat_axis=0, tiled...  125 us
    all_gather x1, waiting for transfers between devices, on_device(): all_queries = lax.all_gather(own_queries, 'cp', axis=0, tiled=True)  115 us
    all_gather x1, waiting for transfers between devices, on_device(): lax.all_gather(arrived, 'grp', axis=0, tiled=True)  44.3 us
    cond x1, other arithmetic  29.2 us
    all_gather x1, blocking collectives, on_device(): mixed = lax.all_gather(mixed_part, 'grp', axis=2, tiled=True)  27.7 us
  transfers between devices with their start and end apart: 9, of which 8 were waited for; matrix products, arithmetic and copies ran while one was open for 2% of the time, Pallas kernels for 0%

commit v1 on v0

v1 whole, which is shorter than its diff:
```python
import math

import jax
import jax.numpy as jnp
from jax import lax
from jax.experimental import pallas as pl
from jax.experimental.pallas import tpu as pltpu
from jax.sharding import PartitionSpec as P

D = 7168
KVL = 512
DV = 128
SPLIT = 4
QROWS = 32
CTX_DEV = 2048
QK = 576
QPAD = 640
SEQS = 3
EXPERTS = 8
QUARTER = D // 4
HALF = QUARTER // 2
N_CP = 32
CTX = CTX_DEV * N_CP

SCALE = 192.0 ** (-0.5)
SCALE2 = SCALE * math.log2(math.e)
MESH = pl.DeviceIdType.MESH
F32 = jnp.float32
BF16 = jnp.bfloat16


def place():
    g = lax.axis_index("grp")
    c = lax.axis_index("cp")
    return g, c, c // 8, (c // 2) % 4, c % 2


def mm(a, b):
    return jnp.dot(a, b, preferred_element_type=F32)


def mm_nt(a, b):
    return lax.dot_general(a, b, (((1,), (1,)), ((), ())), preferred_element_type=F32)


def iota(shape, axis):
    return lax.broadcasted_iota(jnp.int32, shape, axis)


class Wire:
    def __init__(self, send_sems, recv_sems):
        self.send_sems, self.recv_sems = send_sems, recv_sems
        self.started = []

    def push(self, src, dst, device):
        at = len(self.started)
        copy = pltpu.make_async_remote_copy(
            src_ref=src,
            dst_ref=dst,
            send_sem=self.send_sems.at[at],
            recv_sem=self.recv_sems.at[at],
            device_id=device,
            device_id_type=MESH,
        )
        copy.start()
        self.started.append(copy)
        return copy

    def finish(self):
        for copy in self.started:
            copy.wait_send()


def greet(peers):
    barrier = pltpu.get_barrier_semaphore()
    for peer in peers:
        pl.semaphore_signal(barrier, inc=1, device_id=peer, device_id_type=MESH)
    pl.semaphore_wait(barrier, len(peers))


def padded_row(shape, axis, part):
    r = iota(shape, axis)
    s, z, b, a = r % 4, (r // 4) % 2, (r // 8) % 4, r // 32
    x, y = (a, b) if part == 0 else (b, a)
    return s, (x * 4 + y) * 2 + z


def unpack(value):
    value = value.reshape(48, QPAD).astype(F32)
    aux = value[:, KVL:]
    lane = iota(aux.shape, 1)
    peak = jnp.sum(jnp.where(lane == 0, aux, 0.0), axis=-1, keepdims=True)
    total = jnp.sum(jnp.where((lane == 1) | (lane == 2), aux, 0.0), axis=-1, keepdims=True)
    return value[:, :KVL], peak, total


def aux_lanes(peak, total):
    lane = iota((peak.shape[0], QPAD - KVL), 1)
    high = total.astype(BF16).astype(F32)
    low = total - high
    return jnp.where(
        lane == 0, peak, jnp.where(lane == 1, high, jnp.where(lane == 2, low, 0.0))
    )


def merge(values):
    items = [unpack(value) for value in values]
    peak = items[0][1]
    for item in items[1:]:
        peak = jnp.maximum(peak, item[1])
    out, total = None, None
    for item in items:
        factor = jnp.exp((item[1] - peak) * SCALE)
        if out is None:
            out, total = item[0] * factor, item[2] * factor
        else:
            out, total = out + item[0] * factor, total + item[2] * factor
    return out, peak, total


def put(ref, merged):
    out, peak, total = merged
    ref[..., :KVL] = out.astype(BF16).reshape(3, 16, KVL)
    ref[..., KVL:] = aux_lanes(peak, total).astype(BF16).reshape(3, 16, QPAD - KVL)


def attend_kernel(
    q_ref, cache_ref, lat_ref, fac_ref,
    qbuf, kv, kpe, score_a, score_b, prob_a, prob_b, oscr, msg, rx1, rx2, rx3, fin, rxz,
    send_sems, recv_sems, local_sems,
):
    g, c, x, y, z = place()
    up = lambda v, d: lax.rem(v + d, 4)

    def at(px, py, pz):
        return (g, (px * 4 + py) * 2 + pz)

    partner = (lax.rem(g + 2, 4), (x * 4 + y) * 2 + (1 - z))
    own = [
        pltpu.make_async_copy(q_ref.at[h], qbuf.at[h, x, y, z], local_sems.at[h]) for h in range(2)
    ]
    for copy in own:
        copy.start()
    loads = [
        pltpu.make_async_copy(cache_ref.at[s], kv.at[s], local_sems.at[2 + s]) for s in range(3)
    ]
    for copy in loads:
        copy.start()

    greet([at(up(x, d), y, z) for d in (1, 2, 3)] + [at(x, up(y, d), z) for d in (1, 2, 3)] + [partner])
    wire = Wire(send_sems, recv_sems)

    zs = [wire.push(q_ref.at[h], qbuf.at[h, x, y, z], partner) for h in range(2)]
    for copy in own:
        copy.wait()
    for copy in loads:
        copy.wait()
    kpe[...] = jnp.zeros_like(kpe)
    for s in range(3):
        kpe[s, :, : QK - KVL] = kv[s, :, KVL:]
    dirs = (1, 3)
    gathers = []
    for h in range(2):
        zs[h].wait_recv()
        first = []
        for d in dirs:
            first.append(wire.push(qbuf.at[h, x, y, 0], qbuf.at[h, x, y, 0], at(up(x, d), y, z)))
            first.append(wire.push(qbuf.at[h, x, y, 1], qbuf.at[h, x, y, 1], at(x, up(y, d), z)))
        gathers.append(first)
    forwards = []
    for h in range(2):
        for copy in gathers[h]:
            copy.wait_recv()
        second = []
        for d, lanes in ((1, pl.ds(0, 256)), (3, pl.ds(256, 384))):
            rear = up(x, 4 - d)
            ref = qbuf.at[h, rear, y, 0, :, :, lanes]
            second.append(wire.push(ref, ref, at(up(x, d), y, z)))
            rear = up(y, 4 - d)
            ref = qbuf.at[h, x, rear, 1, :, :, lanes]
            second.append(wire.push(ref, ref, at(x, up(y, d), z)))
        forwards.append(second)
    gathers = []
    for h in range(2):
        for copy in forwards[h]:
            copy.wait_recv()
        third = []
        for d in dirs:
            ref = qbuf.at[h, :, y, 0]
            third.append(wire.push(ref, ref, at(x, up(y, d), z)))
            ref = qbuf.at[h, x, :, 1]
            third.append(wire.push(ref, ref, at(up(x, d), y, z)))
        gathers.append(third)
    forwards = []
    for h in range(2):
        for copy in gathers[h]:
            copy.wait_recv()
        fourth = []
        for d, pair in ((1, pl.ds(0, 2)), (3, pl.ds(2, 2))):
            ref = qbuf.at[h, pair, up(y, 4 - d), 0]
            fourth.append(wire.push(ref, ref, at(x, up(y, d), z)))
            ref = qbuf.at[h, up(x, 4 - d), pair, 1]
            fourth.append(wire.push(ref, ref, at(up(x, d), y, z)))
        forwards.append(fourth)

    def scores(h, s, part, score):
        q = qbuf[h, 2 * part : 2 * part + 2, :, :, s].reshape(256, QPAD)
        for n in range(4):
            keys = pl.ds(n * 512, 512)
            value = mm_nt(q[:, :KVL], kv[s, keys, :KVL]) + mm_nt(q[:, KVL:], kpe[s, keys])
            if n < 3:
                score[:, keys] = value
            else:
                score[:, 1536:1920] = value[:, :384]
                row = 16 * part + iota((256, 128), 0) // 16
                position = c * CTX_DEV + 1920 + iota((256, 128), 1)
                score[:, 1920:] = jnp.where(
                    position <= CTX - QROWS + row, value[:, 384:], -1e30
                )

    def weigh(h, s, part, score, prob):
        peak = jnp.max(score[...], axis=-1, keepdims=True).astype(BF16).astype(F32)
        total = jnp.zeros((256, 128), F32)
        for n in range(4):
            keys = pl.ds(n * 512, 512)
            weight = jnp.exp2((score[:, keys] - peak) * SCALE2)
            for m in range(4):
                total = total + weight[:, m * 128 : (m + 1) * 128]
            prob[:, keys] = weight.astype(BF16)
        total = jnp.sum(total, axis=-1, keepdims=True)
        out = mm(prob[...], kv[s, :, :KVL])
        for m in range(4):
            oscr[part, m] = out[:, m * 128 : (m + 1) * 128]
        oscr[part, 4] = aux_lanes(peak, total)
        for n in range(16):
            a, b = (n // 4, n % 4) if part == 0 else (n % 4, n // 4)
            for m in range(5):
                lanes = pl.ds(m * 128, 128)
                msg[h, part, a, b, s, :, lanes] = oscr[part, m, pl.ds(n, 16, stride=16), :].astype(BF16)

    def attend(h):
        @pl.loop(0, SEQS)
        def _(s):
            scores(h, s, 0, score_a)
            scores(h, s, 1, score_b)
            weigh(h, s, 0, score_a, prob_a)
            weigh(h, s, 1, score_b, prob_b)

    axes = [
        (x, y, lambda f, e: at(f, e, z)),
        (y, x, lambda f, e: at(e, f, z)),
    ]

    def reduce_1(h):
        copies = []
        for part, (f, e, to) in enumerate(axes):
            far = up(f, 2)
            for at_, d in enumerate((1, 3)):
                copies.append(
                    wire.push(
                        msg.at[h, part, far, pl.ds(2 * at_, 2)], rx1.at[h, part, at_], to(up(f, d), e)
                    )
                )
        return copies

    def reduce_2(h, copies):
        for copy in copies:
            copy.wait_recv()
        copies = []
        for part, (f, e, to) in enumerate(axes):
            for at_, d in enumerate((1, 3)):
                chunk = up(f, d)

                @pl.loop(0, 2)
                def _(j):
                    put(
                        msg.at[h, part, chunk, 2 * at_ + j],
                        merge([msg[h, part, chunk, 2 * at_ + j], rx1[h, part, at_, j]]),
                    )

                copies.append(
                    wire.push(msg.at[h, part, chunk], rx2.at[h, part, at_], to(chunk, e))
                )
        return copies

    def reduce_3(h, copies):
        for copy in copies:
            copy.wait_recv()
        copies = []
        for part, (f, e, to) in enumerate(axes):

            @pl.loop(0, 4)
            def _(j):
                put(
                    msg.at[h, part, f, j],
                    merge([msg[h, part, f, j], rx2[h, part, 0, j], rx2[h, part, 1, j]]),
                )

            for d in (1, 2, 3):
                copies.append(
                    wire.push(
                        msg.at[h, part, f, up(e, d)], rx3.at[h, part, d - 1], to(f, up(e, d))
                    )
                )
        return copies

    def reduce_4(h, copies):
        for copy in copies:
            copy.wait_recv()
        for part, (f, e, to) in enumerate(axes):
            put(
                fin.at[h, part],
                merge([msg[h, part, f, e]] + [rx3[h, part, d] for d in range(3)]),
            )

    for h in range(2):
        for copy in forwards[h]:
            copy.wait_recv()
    attend(0)
    attend(1)
    steps = [reduce_1(0), reduce_1(1)]
    steps = [reduce_2(h, steps[h]) for h in range(2)]
    steps = [reduce_3(h, steps[h]) for h in range(2)]
    for h in range(2):
        reduce_4(h, steps[h])
    last = wire.push(fin.at[1 - z], rxz, partner)

    for part in range(2):
        picked = jnp.zeros((128, 128), F32)
        for s in range(SEQS):
            seq, row = padded_row((128, 512), 0, part)
            j = iota((128, 512), 1)
            pick = ((seq == s) & (j == row * 16)).astype(F32).astype(BF16)
            picked = picked + mm(pick, qbuf[0, :, :, :, s, :, KVL:].reshape(512, 128))
        lane = iota((128, 128), 1)
        chosen = jnp.sum(
            jnp.where(lane == QK - KVL + c // SPLIT, picked, 0.0), axis=-1, keepdims=True
        )
        fac_ref[part] = jnp.broadcast_to(chosen, (128, 128))

    last.wait_recv()
    for part in range(2):
        out, peak, total = merge([fin[z, part], rxz[part]])
        lat_ref[part * 48 : (part + 1) * 48, :] = (out / total).astype(BF16)
    wire.finish()


def tail_kernel(
    lat_ref, fac_ref, vup_ref, wout_ref, resid_ref, gain_ref, wg_ref, wu_ref, wd_ref, out_ref,
    vup, wout, wg, wu, wd, heads, pbuf, rxa, ebuf, rxb, zbuf, rxc, hid, hidf,
    sq, rxs, gs, rxg, units, qbuf, rxq, ybuf, rxy, wbuf, rxw, fo,
    send_sems, recv_sems, local_sems,
):
    g, c, x, y, z = place()
    up = lambda v, d: lax.rem(v + d, 4)

    def at(px, py, pz):
        return (g, (px * 4 + py) * 2 + pz)

    columns = pl.ds(pl.multiple_of(g * QUARTER, 128), QUARTER)
    loads = [
        pltpu.make_async_copy(src, dst, local_sems.at[n])
        for n, (src, dst) in enumerate(
            (
                (vup_ref.at[g], vup),
                (wout_ref.at[:, columns], wout),
                (wg_ref.at[0], wg),
                (wu_ref.at[0], wu),
                (wd_ref.at[0], wd),
            )
        )
    ]
    for copy in loads:
        copy.start()
    mates = [(up(g, d), c) for d in (1, 2, 3)]
    far = at(x, y, 1 - z)
    greet(
        [at(up(x, d), y, z) for d in (1, 2, 3)]
        + [at(x, up(y, d), z) for d in (1, 2, 3)]
        + [far]
        + mates
    )
    wire = Wire(send_sems, recv_sems)
    axes = [
        (x, y, lambda f, e: at(f, e, z)),
        (y, x, lambda f, e: at(e, f, z)),
    ]

    loads[0].wait()
    heads[g] = mm(lat_ref[...], vup[...]).astype(BF16)
    copies = [wire.push(heads.at[g], heads.at[g], mate) for mate in mates]
    spread, gathered = [], []
    for part in range(2):
        seq, row = padded_row((128, 96), 0, part)
        j = iota((128, 96), 1)
        spread.append(
            ((seq < SEQS) & (j == (row // 16) * 48 + seq * 16 + row % 16)).astype(F32).astype(BF16)
        )
        seq, row = padded_row((96, 128), 1, part)
        j = iota((96, 128), 0)
        gathered.append(
            ((seq < SEQS) & (j == (row // 16) * 48 + seq * 16 + row % 16)).astype(F32).astype(BF16)
        )
    for copy in copies:
        copy.wait_recv()
    loads[1].wait()
    for part in range(2):
        cols = pl.ds(part * HALF, HALF)
        seq, row = padded_row((128, 16), 0, part)
        mine = ((row == c) & (seq == iota((128, 16), 1)) & (seq < SEQS)).astype(F32).astype(BF16)
        value = mm(mine, resid_ref[:, cols])
        for k in range(4):
            rows = mm(spread[part], heads[k]).astype(BF16)
            value = value + mm(rows, wout[k * DV : (k + 1) * DV, cols])
        pbuf[part] = value.astype(BF16).reshape(4, 32, HALF)

    def scatter(source, landing):
        copies = []
        for part, (f, e, to) in enumerate(axes):
            for d in (1, 2, 3):
                copies.append(
                    wire.push(source.at[part, up(f, d)], landing.at[part, d - 1], to(up(f, d), e))
                )
        return copies

    def summed(first, landing, part):
        value = first.astype(F32)
        for d in range(3):
            value = value + landing[part, d].astype(F32)
        return value

    copies = scatter(pbuf, rxa)
    for copy in copies:
        copy.wait_recv()
    copies = []
    for part, (f, e, to) in enumerate(axes):
        ebuf[part] = summed(pbuf[part, f], rxa, part).astype(BF16)
        for d in (1, 2, 3):
            copies.append(wire.push(ebuf.at[part], rxb.at[part, d - 1], to(f, up(e, d))))
    for copy in copies:
        copy.wait_recv()
    for part in range(2):
        zbuf[part] = summed(ebuf[part], rxb, part).astype(BF16)
    copy = wire.push(zbuf, rxc, far)
    copy.wait_recv()
    copies = []
    for part, (f, e, to) in enumerate(axes):
        value = (zbuf[part].astype(F32) + rxc[part].astype(F32)).astype(BF16)
        hid[part, f] = value
        hidf[part] = value.astype(F32).reshape(4, 8, HALF)
        for d in (1, 2, 3):
            ref = hid.at[part, f]
            copies.append(wire.push(ref, ref, to(up(f, d), e)))
    for copy in copies:
        copy.wait_recv()

    loads[2].wait()
    loads[3].wait()
    eye = iota((96, 128), 0) == iota((96, 128), 1)
    squares = jnp.zeros((96, 1), F32)
    gate = jnp.zeros((96, 512), F32)
    rise = jnp.zeros((96, 512), F32)
    for part in range(2):
        rows = mm(gathered[part], hid[part].reshape(128, HALF))
        squares = squares + jnp.sum(rows * rows, axis=-1, keepdims=True)
        cols = pl.ds(part * HALF, HALF)
        scaled = (rows * gain_ref[0:1, cols]).astype(BF16)
        gate = gate + mm(scaled, wg[cols, :])
        rise = rise + mm(scaled, wu[cols, :])
    sq[...] = jnp.broadcast_to(
        jnp.sum(jnp.where(eye, squares, 0.0), axis=0, keepdims=True), (8, 128)
    )
    for j in range(4):
        gs[j, :, :128] = gate[:, j * 128 : (j + 1) * 128].astype(BF16)
        gs[j, :, 128:] = rise[:, j * 128 : (j + 1) * 128].astype(BF16)
    copies = []
    for d in (1, 2, 3):
        copies.append(wire.push(sq, rxs.at[d - 1], mates[d - 1]))
        copies.append(wire.push(gs.at[up(g, d)], rxg.at[d - 1], mates[d - 1]))
    for copy in copies:
        copy.wait_recv()
    both = gs[g].astype(F32)
    total = sq[0:1, :]
    for d in range(3):
        both = both + rxg[d].astype(F32)
        total = total + rxs[d, 0:1, :]
    total = jnp.sum(jnp.where(eye, total, 0.0), axis=-1, keepdims=True)
    both = both * lax.rsqrt(total * (1.0 / D) + 1e-06)
    gate, rise = both[:, :128], both[:, 128:]
    units[g] = (gate / (1.0 + jnp.exp(-gate)) * rise).astype(BF16)
    copies = [wire.push(units.at[g], units.at[g], mate) for mate in mates]
    for copy in copies:
        copy.wait_recv()
    loads[4].wait()
    for part in range(2):
        cols = pl.ds(part * HALF, HALF)
        value = jnp.zeros((128, HALF), F32)
        for k in range(4):
            rows = mm(spread[part], units[k]).astype(BF16)
            value = value + mm(rows, wd[k * 128 : (k + 1) * 128, cols])
        value = value.astype(BF16).astype(F32) * fac_ref[part, :, 0:1]
        qbuf[part] = value.astype(BF16).reshape(4, 32, HALF)
    copies = scatter(qbuf, rxq)
    for copy in copies:
        copy.wait_recv()
    copies = []
    for part, (f, e, to) in enumerate(axes):
        ybuf[part] = summed(qbuf[part, f], rxq, part).reshape(4, 8, HALF)
        for d in (1, 2, 3):
            copies.append(wire.push(ybuf.at[part, up(e, d)], rxy.at[part, d - 1], to(f, up(e, d))))
    for copy in copies:
        copy.wait_recv()
    for part, (f, e, to) in enumerate(axes):
        wbuf[part] = summed(ybuf[part, e], rxy, part)
    copy = wire.push(wbuf, rxw, far)
    copy.wait_recv()
    for part, (f, e, to) in enumerate(axes):
        value = hidf[part, e] + (wbuf[part] + rxw[part])
        fo[g, part * 4 : (part + 1) * 4, :] = jnp.where(z == 0, value[0:4], value[4:8])
    copies = [wire.push(fo.at[g], fo.at[g], mate) for mate in mates]
    for copy in copies:
        copy.wait_recv()
    for k in range(4):
        for part in range(2):
            at_ = k * QUARTER + part * HALF
            out_ref[:, at_ : at_ + HALF] = fo[k, part * 4 : part * 4 + SEQS, :].astype(BF16)
    wire.finish()


def vmem():
    return pl.BlockSpec(memory_space=pltpu.VMEM)


def hbm():
    return pl.BlockSpec(memory_space=pl.ANY)


def on_device(
    queries, cache, value_up_weight, w_out, resid, norm_gain, routes, route_weight,
    w_gate, w_up, w_down,
):
    g, c, x, y, z = place()
    pair, core = lax.rem(g // 2 + z, 2), g % 2
    by_column = queries.reshape(SEQS, 16, 8, QK)
    lower = lax.dynamic_index_in_dim(by_column, 2 * pair + core, 2, keepdims=False)
    upper = lax.dynamic_index_in_dim(by_column, 4 + 2 * (1 - pair) + core, 2, keepdims=False)
    matches = routes[:, 0, :, None] == jnp.arange(EXPERTS, dtype=jnp.int32)
    weights = jnp.sum(
        jnp.where(matches, route_weight[:, 0, :, None].astype(F32), 0.0), axis=1
    ).astype(BF16)
    spare = jnp.pad(weights, ((0, 0), (0, QPAD - QK - EXPERTS)))
    spare = jnp.broadcast_to(spare[None, :, None, :], (2, SEQS, 16, QPAD - QK))
    rows = jnp.concatenate([jnp.stack([lower, upper]), spare], axis=-1)

    latent, factor = pl.pallas_call(
        attend_kernel,
        out_shape=(
            jax.ShapeDtypeStruct((96, KVL), BF16),
            jax.ShapeDtypeStruct((2, 128, 128), F32),
        ),
        in_specs=[vmem(), hbm()],
        out_specs=(vmem(), vmem()),
        scratch_shapes=[
            pltpu.VMEM((2, 4, 4, 2, SEQS, 16, QPAD), BF16),
            pltpu.VMEM((SEQS, CTX_DEV, QK), BF16),
            pltpu.VMEM((SEQS, CTX_DEV, 128), BF16),
            pltpu.VMEM((256, CTX_DEV), F32),
            pltpu.VMEM((256, CTX_DEV), F32),
            pltpu.VMEM((256, CTX_DEV), BF16),
            pltpu.VMEM((256, CTX_DEV), BF16),
            pltpu.VMEM((2, 5, 256, 128), F32),
            pltpu.VMEM((2, 2, 4, 4, SEQS, 16, QPAD), BF16),
            pltpu.VMEM((2, 2, 2, 2, SEQS, 16, QPAD), BF16),
            pltpu.VMEM((2, 2, 2, 4, SEQS, 16, QPAD), BF16),
            pltpu.VMEM((2, 2, 3, SEQS, 16, QPAD), BF16),
            pltpu.VMEM((2, 2, SEQS, 16, QPAD), BF16),
            pltpu.VMEM((2, SEQS, 16, QPAD), BF16),
            pltpu.SemaphoreType.DMA((64,)),
            pltpu.SemaphoreType.DMA((64,)),
            pltpu.SemaphoreType.DMA((5,)),
        ],
        compiler_params=pltpu.CompilerParams(
            collective_id=0, has_side_effects=True, vmem_limit_bytes=56 * 1024 * 1024
        ),
    )(rows, cache)

    own_resid = lax.dynamic_slice_in_dim(resid[:, 0], g * QUARTER, QUARTER, 1)
    own_resid = jnp.pad(own_resid, ((0, 16 - SEQS), (0, 0)))
    own_gain = lax.dynamic_slice_in_dim(norm_gain, g * QUARTER, QUARTER, 0)
    own_gain = jnp.broadcast_to(own_gain[None], (8, QUARTER))
    mixed = pl.pallas_call(
        tail_kernel,
        out_shape=jax.ShapeDtypeStruct((SEQS, D), BF16),
        in_specs=[vmem(), vmem(), hbm(), hbm(), vmem(), vmem(), hbm(), hbm(), hbm()],
        out_specs=vmem(),
        scratch_shapes=[
            pltpu.VMEM((KVL, DV), BF16),
            pltpu.VMEM((512, QUARTER), BF16),
            pltpu.VMEM((QUARTER, 512), BF16),
            pltpu.VMEM((QUARTER, 512), BF16),
            pltpu.VMEM((512, QUARTER), BF16),
            pltpu.VMEM((4, 96, DV), BF16),
            pltpu.VMEM((2, 4, 32, HALF), BF16),
            pltpu.VMEM((2, 3, 32, HALF), BF16),
            pltpu.VMEM((2, 32, HALF), BF16),
            pltpu.VMEM((2, 3, 32, HALF), BF16),
            pltpu.VMEM((2, 32, HALF), BF16),
            pltpu.VMEM((2, 32, HALF), BF16),
            pltpu.VMEM((2, 4, 32, HALF), BF16),
            pltpu.VMEM((2, 4, 8, HALF), F32),
            pltpu.VMEM((8, 128), F32),
            pltpu.VMEM((3, 8, 128), F32),
            pltpu.VMEM((4, 96, 256), BF16),
            pltpu.VMEM((3, 96, 256), BF16),
            pltpu.VMEM((4, 96, 128), BF16),
            pltpu.VMEM((2, 4, 32, HALF), BF16),
            pltpu.VMEM((2, 3, 32, HALF), BF16),
            pltpu.VMEM((2, 4, 8, HALF), F32),
            pltpu.VMEM((2, 3, 8, HALF), F32),
            pltpu.VMEM((2, 8, HALF), F32),
            pltpu.VMEM((2, 8, HALF), F32),
            pltpu.VMEM((4, 8, HALF), F32),
            pltpu.SemaphoreType.DMA((50,)),
            pltpu.SemaphoreType.DMA((50,)),
            pltpu.SemaphoreType.DMA((5,)),
        ],
        compiler_params=pltpu.CompilerParams(
            collective_id=1, has_side_effects=True, vmem_limit_bytes=40 * 1024 * 1024
        ),
    )(latent, factor, value_up_weight, w_out, own_resid, own_gain, w_gate, w_up, w_down)
    return mixed.reshape(SEQS, 1, D)


def solution(mesh):
    placed = (
        P(None, "cp", None),
        P(None, "cp", None),
        P("cp", None, None),
        P("cp", None),
        P(None, "cp", None),
        P(),
        P(None, "cp", None),
        P(None, "cp", None),
        P("cp", "grp", None),
        P("cp", "grp", None),
        P("cp", None, "grp"),
    )
    return jax.shard_map(
        on_device, mesh=mesh, in_specs=placed, out_specs=P(None, "cp", None), check_vma=False
    )
```

time: 1220 us -> 168 us (0.14)
  waiting for transfers between devices: 961 us -> 0 us
  Pallas kernels: 0 us -> 143 us
  other arithmetic: 63.2 us -> 1.51 us
  matrix products: 58.9 us -> 0 us
  blocking collectives: 55.9 us -> 0 us
  starting transfers between devices: 28.1 us -> 0 us
  local copies, waits for them, and re-layouts: 39 us -> 22.1 us
  between operations: 14.8 us -> 0.09 us
    unnamed x7 -> x0, waiting for transfers between devices: 650 us -> none
    all_gather x2 -> x0, waiting for transfers between devices: 160 us -> none  [the longest x1 115 us: on_device(): all_queries = lax.all_gather(own_queries, 'cp', axis=0, tiled=True)]
    pallas_call x0 -> x2, Pallas kernels: none -> 143 us  [the longest x1 83 us: on_device(): pl.pallas_call(attend_kernel, out_shape=(jax.ShapeDtypeStruct((96, KVL),...]
    all_to_all x4 -> x0, waiting for transfers between devices: 138 us -> none  [the longest x1 125 us: on_device(): lax.all_to_all(row_output[None], 'cp', split_axis=2, concat_axis=0, tiled...]
    dot_general x7 -> x0, matrix products: 58.9 us -> none  [the longest x1 23.9 us: attend_latent(): jnp.einsum('qht,tv->qhv', weights_exp.astype(jnp.bfloat16), key_rows[:, :...]
    all_gather x2 -> x0, blocking collectives: 33.1 us -> none  [the longest x1 27.7 us: on_device(): mixed = lax.all_gather(mixed_part, 'grp', axis=2, tiled=True)]
    cond x1 -> x0, other arithmetic: 29.2 us -> none
    all_to_all x4 -> x0, starting transfers between devices: 27.8 us -> none  [the longest x1 9.36 us: on_device(): lax.all_to_all(row_output[None], 'cp', split_axis=2, concat_axis=0, tiled...]
  transfers between devices with their start and end apart: 9 -> 0, of which waited for: 8 -> 0; matrix products, arithmetic and copies ran while one was open for 2% -> 0% of each run, Pallas kernels for 0% -> 0%
where the time goes in v1:
time: 168 us; the launch traced here: 167 us
  Pallas kernels  143 us (85%)
  local copies, waits for them, and re-layouts  22.1 us (13%)
    pallas_call x1, Pallas kernels, on_device(): pl.pallas_call(attend_kernel, out_shape=(jax.ShapeDtypeStruct((96, KVL),...  83 us
    pallas_call x1, Pallas kernels, on_device(): pl.pallas_call(tail_kernel, out_shape=jax.ShapeDtypeStruct((SEQS, D), BF1...  60.5 us
    unnamed x19, local copies, waits for them, and re-layouts  19.4 us

profile of v1, /device:TPU:1, one launch (start us, length us, event | category | flops | bytes accessed | tf_op | source)
XLA Modules:
  0.0 167.2 jit_solution(8677775784578588161)
XLA Ops:
  0.0 0.0 copy-start
  0.0 1.6 reshape.21
  1.6 0.3 constant_dynamic-slice_fusion.1
  1.9 0.7 copy.24
  2.6 0.7 bitcast_convert_fusion
  3.3 0.1 select_reduce_fusion
  3.4 0.7 pad_maximum_fusion.q_ref
  4.2 10.2 %copy.17.cache_ref = bf16[3,2048,576]{2,1,0:T(8,128)(2,1)} copy(bf16[3,2048,576]{1,2,0:T(8,128)(2,1)} %param.12) | data formatting | bytes 14155776 | tf_op args[1]
  14.3 0.0 copy-start.2
  14.3 0.0 copy-start.5
  14.3 83.0 %shard_map.109 = (bf16[96,512]{1,0:T(8,128)(2,1)}, f32[2,128,128]{2,1,0:T(8,128)}) custom-call(bf16[2,3,16,640]{3,2,1,0:T(8,128)(2,1)} %pad_maximum_fusion.q_ref, bf16[3,2048,576]{2,1,0:T(8,128)(2,1)} %copy.17.cache_ref), custom_call_target="tpu_custom_call" | custom-call | tf_op jit(solution)/shard_map/pallas_call | solution.py:555
  97.3 0.0 copy-done
  97.4 0.8 dynamic_slice.19
  98.2 0.0 copy-done.2
  98.2 0.0 copy-done.5
  98.2 0.0 copy-start.1
  98.2 3.1 %copy-done.1 = bf16[512,7168]{1,0:T(8,128)(2,1)S(1)} copy-done((bf16[512,7168]{1,0:T(8,128)(2,1)S(1)}, bf16[512,7168]{1,0:T(8,128)(2,1)}, u32[]{:S(2)}) %copy-start.1) | copy-done | bytes 7340056
  101.3 0.0 copy-start.3
  101.3 1.5 copy-done.3
  102.8 0.0 copy-start.4
  102.8 1.5 copy-done.4
  104.3 0.0 copy-start.6
  104.3 0.9 copy-done.6
  105.2 0.0 copy-start.7
  105.2 0.9 copy-done.7
  106.1 60.5 %shard_map.110 = bf16[3,7168]{1,0:T(4,128)(2,1)S(1)} custom-call(bf16[96,512]{1,0:T(8,128)(2,1)S(1)} %copy-done.7, f32[2,128,128]{2,1,0:T(8,128)S(1)} %copy-done.6, bf16[4,512,128]{2,1,0:T(8,128)(2,1)S(1)} %copy-done.5, bf16[512,7168]{1,0:T(8,128)(2,1)S(1)} %copy-done.1, bf16[16,1792]{1,0:T(8,128)(2,1)S(1)} %pad.9.resid_ref, ...), custom_call_target="tpu_custom_call" | custom-call | tf_op jit(solution)/shard_map/pallas_call | solution.py:591
  166.6 0.6 copy.26
  (6 shorter events, 0.1 us)
Async XLA Ops:
  0.0 97.3 %copy-start = (bf16[3,1,7168]{2,0,1:T(4,128)(2,1)S(1)}, bf16[3,1,7168]{2,0,1:T(4,128)(2,1)}, u32[]{:S(2)}) copy-start(bf16[3,1,7168]{2,0,1:T(4,128)(2,1)} %param.15) | copy-start | bytes 129028
  14.3 83.9 %copy-start.2 = (bf16[1,1792,512]{2,1,0:T(8,128)(2,1)S(1)}, bf16[1,1792,512]{2,1,0:T(8,128)(2,1)}, u32[]{:S(2)}) copy-start(bf16[1,1792,512]{2,1,0:T(8,128)(2,1)} %wg_ref.1) | copy-start | bytes 5505028
  14.3 83.9 %copy-start.5 = (bf16[4,512,128]{2,1,0:T(8,128)(2,1)S(1)}, bf16[4,512,128]{2,1,0:T(8,128)(2,1)}, u32[]{:S(2)}) copy-start(bf16[4,512,128]{2,1,0:T(8,128)(2,1)} %vup_ref.1) | copy-start | bytes 1572868
  98.2 3.1 %copy-start.1 = (bf16[512,7168]{1,0:T(8,128)(2,1)S(1)}, bf16[512,7168]{1,0:T(8,128)(2,1)}, u32[]{:S(2)}) copy-start(bf16[512,7168]{1,0:T(8,128)(2,1)} %wout_ref.1) | copy-start | bytes 22020100
  101.3 1.5 copy-start.3
  102.8 1.5 copy-start.4
  104.3 0.9 copy-start.6
  105.2 0.9 copy-start.7

commit v2 on v1

v2 whole, which is shorter than its diff:
```python
import math

import jax
import jax.numpy as jnp
from jax import lax
from jax.experimental import pallas as pl
from jax.experimental.pallas import tpu as pltpu
from jax.sharding import PartitionSpec as P

D = 7168
KVL = 512
DV = 128
SPLIT = 4
QROWS = 32
CTX_DEV = 2048
QK = 576
QPAD = 640
SEQS = 3
EXPERTS = 8
QUARTER = D // 4
HALF = QUARTER // 2
N_CP = 32
CTX = CTX_DEV * N_CP

SCALE = 192.0 ** (-0.5)
SCALE2 = SCALE * math.log2(math.e)
MESH = pl.DeviceIdType.MESH
F32 = jnp.float32
BF16 = jnp.bfloat16


def place():
    g = lax.axis_index("grp")
    c = lax.axis_index("cp")
    return g, c, c // 8, (c // 2) % 4, c % 2


def mm(a, b):
    return jnp.dot(a, b, preferred_element_type=F32)


def mm_nt(a, b):
    return lax.dot_general(a, b, (((1,), (1,)), ((), ())), preferred_element_type=F32)


def iota(shape, axis):
    return lax.broadcasted_iota(jnp.int32, shape, axis)


def part_of(ref, *index):
    return ref.at[index] if index else ref


class Wire:
    def __init__(self, send_sems, recv_sems):
        self.send_sems, self.recv_sems = send_sems, recv_sems
        self.started = []

    def push(self, src, dst, device):
        copy = Copy(self, len(self.started), src, dst, device)
        self.started.append(copy)
        copy.make().start()
        return copy

    def finish(self):
        for copy in self.started:
            copy.make().wait_send()


class Copy:
    def __init__(self, wire, at, src, dst, device):
        self.wire, self.at, self.src, self.dst, self.device = wire, at, src, dst, device

    def make(self):
        return pltpu.make_async_remote_copy(
            src_ref=part_of(*self.src),
            dst_ref=part_of(*self.dst),
            send_sem=self.wire.send_sems.at[self.at],
            recv_sem=self.wire.recv_sems.at[self.at],
            device_id=self.device,
            device_id_type=MESH,
        )

    def wait_recv(self):
        self.make().wait_recv()


def arrive(copies):
    for copy in copies:
        copy.wait_recv()


def greet(peers):
    barrier = pltpu.get_barrier_semaphore()
    for peer in peers:
        pl.semaphore_signal(barrier, inc=1, device_id=peer, device_id_type=MESH)
    pl.semaphore_wait(barrier, len(peers))


def padded_row(shape, axis, part):
    r = iota(shape, axis)
    s, z, b, a = r % 4, (r // 4) % 2, (r // 8) % 4, r // 32
    x, y = (a, b) if part == 0 else (b, a)
    return s, (x * 4 + y) * 2 + z


def unpack(value):
    value = value.reshape(-1, QPAD).astype(F32)
    aux = value[:, KVL:]
    lane = iota(aux.shape, 1)
    peak = jnp.sum(jnp.where(lane == 0, aux, 0.0), axis=-1, keepdims=True)
    total = jnp.sum(jnp.where((lane == 1) | (lane == 2), aux, 0.0), axis=-1, keepdims=True)
    return value[:, :KVL], peak, total


def aux_lanes(peak, total):
    lane = iota((peak.shape[0], QPAD - KVL), 1)
    high = total.astype(BF16).astype(F32)
    low = total - high
    return jnp.where(
        lane == 0, peak, jnp.where(lane == 1, high, jnp.where(lane == 2, low, 0.0))
    )


def merge(values):
    items = [unpack(value) for value in values]
    peak = items[0][1]
    for item in items[1:]:
        peak = jnp.maximum(peak, item[1])
    out, total = None, None
    for item in items:
        factor = jnp.exp((item[1] - peak) * SCALE)
        if out is None:
            out, total = item[0] * factor, item[2] * factor
        else:
            out, total = out + item[0] * factor, total + item[2] * factor
    return out, peak, total


def put(ref, merged):
    out, peak, total = merged
    ref[..., :KVL] = out.astype(BF16).reshape(2, 16, KVL)
    ref[..., KVL:] = aux_lanes(peak, total).astype(BF16).reshape(2, 16, QPAD - KVL)


def kernel(
    q_ref, cache_ref, vup_ref, wout_ref, resid_ref, gain_ref, wg_ref, wu_ref, wd_ref, out_ref,
    qbuf, kv, score_a, score_b, prob_a, prob_b, oscr, msg, rx1, rx2, rx3, fin, rxz, lat, fac,
    vup, wout, wg, wu, wd, heads, pbuf, rxa, ebuf, rxb, zbuf, rxc, hid, hidf,
    sq, rxs, gs, rxg, units, part_buf, rxq, ybuf, rxy, wbuf, rxw, fo,
    send_sems, recv_sems, local_sems,
):
    g, c, x, y, z = place()
    up = lambda v, d: lax.rem(v + d, 4)

    def at(px, py, pz):
        return (g, (px * 4 + py) * 2 + pz)

    xs = [x] + [up(x, d) for d in (1, 2, 3)]
    ys = [y] + [up(y, d) for d in (1, 2, 3)]
    to_x = [None] + [at(xs[d], y, z) for d in (1, 2, 3)]
    to_y = [None] + [at(x, ys[d], z) for d in (1, 2, 3)]
    partner = (lax.rem(g + 2, 4), (x * 4 + y) * 2 + (1 - z))
    far = at(x, y, 1 - z)
    gs_of = [g] + [up(g, d) for d in (1, 2, 3)]
    mates = [None] + [(gs_of[d], c) for d in (1, 2, 3)]
    columns = pl.ds(pl.multiple_of(g * QUARTER, 128), QUARTER)
    pairs = [(q_ref.at[s], qbuf.at[s, x, y, z]) for s in range(SEQS)]
    pairs += [(cache_ref.at[s], kv.at[s, pl.ds(0, QK)]) for s in range(SEQS)]
    pairs += [
        (vup_ref.at[g], vup),
        (wout_ref.at[:, columns], wout),
        (wg_ref.at[0], wg),
        (wu_ref.at[0], wu),
        (wd_ref.at[0], wd),
    ]
    loads = [
        pltpu.make_async_copy(src, dst, local_sems.at[n]) for n, (src, dst) in enumerate(pairs)
    ]
    for copy in loads:
        copy.start()

    greet(
        to_x[1:] + to_y[1:] + mates[1:] + [partner, far]
    )
    wire = Wire(send_sems, recv_sems)

    dirs = (1, 3)
    other = 1 - z

    def gather_0(s):
        return [wire.push((q_ref, s), (qbuf, s, x, y, z), partner)]

    def gather_1(s, copies):
        arrive(copies)
        copies = []
        for d in dirs:
            ref = (qbuf, s, x, y, 0)
            copies.append(wire.push(ref, ref, to_x[d]))
            ref = (qbuf, s, x, y, 1)
            copies.append(wire.push(ref, ref, to_y[d]))
        return copies

    def gather_2(s, copies):
        arrive(copies)
        copies = []
        for k, d in enumerate(dirs):
            ref = (qbuf, s, xs[4 - d], y, 0, k)
            copies.append(wire.push(ref, ref, to_x[d]))
            ref = (qbuf, s, x, ys[4 - d], 1, k)
            copies.append(wire.push(ref, ref, to_y[d]))
        return copies

    def gather_3(s, copies):
        arrive(copies)
        copies = []
        for d in dirs:
            ref = (qbuf, s, slice(None), y, 0)
            copies.append(wire.push(ref, ref, to_y[d]))
            ref = (qbuf, s, x, slice(None), 1)
            copies.append(wire.push(ref, ref, to_x[d]))
        return copies

    def gather_4(s, copies):
        arrive(copies)
        copies = []
        for k, d in enumerate(dirs):
            ref = (qbuf, s, pl.ds(2 * k, 2), ys[4 - d], 0)
            copies.append(wire.push(ref, ref, to_y[d]))
            ref = (qbuf, s, xs[4 - d], pl.ds(2 * k, 2), 1)
            copies.append(wire.push(ref, ref, to_x[d]))
        return copies

    def scores(s, half, part, score):
        q = qbuf[s, 2 * part : 2 * part + 2, :, :, half].reshape(256, QPAD)
        for n in range(4):
            keys = pl.ds(n * 512, 512)
            value = mm(q, kv[s, :, keys])
            if n < 3:
                score[:, keys] = value
            else:
                score[:, 1536:1920] = value[:, :384]
                row = 16 * part + iota((256, 128), 0) // 16
                position = c * CTX_DEV + 1920 + iota((256, 128), 1)
                score[:, 1920:] = jnp.where(
                    position <= CTX - QROWS + row, value[:, 384:], -1e30
                )

    def weigh(s, half, part, score, prob):
        peak = jnp.max(score[...], axis=-1, keepdims=True).astype(BF16).astype(F32)
        total = jnp.zeros((256, 128), F32)
        for n in range(4):
            keys = pl.ds(n * 512, 512)
            weight = jnp.exp2((score[:, keys] - peak) * SCALE2)
            for m in range(4):
                total = total + weight[:, m * 128 : (m + 1) * 128]
            prob[:, keys] = weight.astype(BF16)
        total = jnp.sum(total, axis=-1, keepdims=True)
        out = mm_nt(prob[...], kv[s, :KVL, :])
        for m in range(4):
            oscr[part, m] = out[:, m * 128 : (m + 1) * 128]
        oscr[part, 4] = aux_lanes(peak, total)
        for n in range(16):
            a, b = (n // 4, n % 4) if part == 0 else (n % 4, n // 4)
            for m in range(5):
                lanes = pl.ds(m * 128, 128)
                msg[s, part, a, b, half, :, lanes] = oscr[
                    part, m, pl.ds(n, 16, stride=16), :
                ].astype(BF16)

    def attend(t):
        s, half = t // 2, t % 2
        scores(s, half, 0, score_a)
        scores(s, half, 1, score_b)
        weigh(s, half, 0, score_a, prob_a)
        weigh(s, half, 1, score_b, prob_b)

    axes = [(xs, ys, to_x, to_y), (ys, xs, to_y, to_x)]

    def reduce_1(s):
        copies = []
        for part, (fs, es, to_f, to_e) in enumerate(axes):
            for k, d in enumerate(dirs):
                src = (msg, s, part, fs[2], pl.ds(2 * k, 2))
                copies.append(wire.push(src, (rx1, s, part, k), to_f[d]))
        return copies

    def reduce_2(s, copies):
        arrive(copies)
        copies = []
        for part, (fs, es, to_f, to_e) in enumerate(axes):
            for k, d in enumerate(dirs):

                @pl.loop(0, 2)
                def _(j):
                    put(
                        msg.at[s, part, fs[d], 2 * k + j],
                        merge([msg[s, part, fs[d], 2 * k + j], rx1[s, part, k, j]]),
                    )

                copies.append(wire.push((msg, s, part, fs[d]), (rx2, s, part, k), to_f[d]))
        return copies

    def reduce_3(s, copies):
        arrive(copies)
        copies = []
        for part, (fs, es, to_f, to_e) in enumerate(axes):

            @pl.loop(0, 4)
            def _(j):
                put(
                    msg.at[s, part, fs[0], j],
                    merge([msg[s, part, fs[0], j], rx2[s, part, 0, j], rx2[s, part, 1, j]]),
                )

            for d in (1, 2, 3):
                src = (msg, s, part, fs[0], es[d])
                copies.append(wire.push(src, (rx3, s, part, d - 1), to_e[d]))
        return copies

    def reduce_4(s, copies):
        arrive(copies)
        for part, (fs, es, to_f, to_e) in enumerate(axes):
            out, peak, total = merge(
                [msg[s, part, fs[0], es[0]]] + [rx3[s, part, d] for d in range(3)]
            )
            fin[s, :, part, :, :KVL] = out.astype(BF16).reshape(2, 16, KVL)
            fin[s, :, part, :, KVL:] = aux_lanes(peak, total).astype(BF16).reshape(
                2, 16, QPAD - KVL
            )
        return [wire.push((fin, s, other), (rxz, s), partner)]

    def reduce_5(s, copies):
        arrive(copies)
        out, peak, total = merge([fin[s, z], rxz[s]])
        lat[s * QROWS : (s + 1) * QROWS, :] = (out / total).astype(BF16)

    zs = [gather_0(s) for s in range(SEQS)]
    for copy in loads[:3]:
        copy.wait()
    got = [None] * SEQS
    got[0] = gather_1(0, zs[0])
    kv[:, QK:, :] = jnp.zeros((SEQS, QPAD - QK, CTX_DEV), BF16)
    got[0] = gather_2(0, got[0])
    got[0] = gather_3(0, got[0])
    got[1] = gather_1(1, zs[1])
    got[0] = gather_4(0, got[0])
    got[1] = gather_2(1, got[1])
    for copy in loads[3:6]:
        copy.wait()
    arrive(got[0])
    got[1] = gather_3(1, got[1])
    red = [None] * SEQS

    @pl.loop(0, 6)
    def _(t):
        @pl.when(t == 1)
        def _():
            got[1] = gather_4(1, got[1])
            got[2] = gather_1(2, zs[2])
            got[2] = gather_2(2, got[2])

        @pl.when(t == 2)
        def _():
            arrive(got[1])
            got[2] = gather_3(2, got[2])
            red[0] = reduce_1(0)

        @pl.when(t == 3)
        def _():
            got[2] = gather_4(2, got[2])
            red[0] = reduce_2(0, red[0])

        @pl.when(t == 4)
        def _():
            arrive(got[2])
            red[0] = reduce_3(0, red[0])
            red[1] = reduce_1(1)

        @pl.when(t == 5)
        def _():
            red[0] = reduce_4(0, red[0])
            red[1] = reduce_2(1, red[1])

        attend(t)

    red[2] = reduce_1(2)
    red[1] = reduce_3(1, red[1])
    red[2] = reduce_2(2, red[2])
    red[1] = reduce_4(1, red[1])
    red[2] = reduce_3(2, red[2])

    for part in range(2):
        picked = jnp.zeros((128, 128), F32)
        for s in range(SEQS):
            seq, row = padded_row((128, 512), 0, part)
            j = iota((128, 512), 1)
            pick = ((seq == s) & (j == row * 16)).astype(F32).astype(BF16)
            picked = picked + mm(pick, qbuf[s, :, :, :, 0, :, KVL:].reshape(512, 128))
        lane = iota((128, 128), 1)
        chosen = jnp.sum(
            jnp.where(lane == QK - KVL + c // SPLIT, picked, 0.0), axis=-1, keepdims=True
        )
        fac[part] = jnp.broadcast_to(chosen, (128, 128))

    red[2] = reduce_4(2, red[2])
    for s in range(SEQS):
        reduce_5(s, red[s])

    loads[6].wait()
    heads[g] = mm(lat[...], vup[...]).astype(BF16)
    copies = [wire.push((heads, g), (heads, g), mates[d]) for d in (1, 2, 3)]
    spread, gathered = [], []
    for part in range(2):
        seq, row = padded_row((128, 96), 0, part)
        j = iota((128, 96), 1)
        spread.append(
            ((seq < SEQS) & (j == seq * QROWS + row)).astype(F32).astype(BF16)
        )
        seq, row = padded_row((96, 128), 1, part)
        j = iota((96, 128), 0)
        gathered.append(
            ((seq < SEQS) & (j == seq * QROWS + row)).astype(F32).astype(BF16)
        )
    arrive(copies)
    loads[7].wait()
    for part in range(2):
        cols = pl.ds(part * HALF, HALF)
        seq, row = padded_row((128, 16), 0, part)
        mine = ((row == c) & (seq == iota((128, 16), 1)) & (seq < SEQS)).astype(F32).astype(BF16)
        value = mm(mine, resid_ref[:, cols])
        for k in range(4):
            rows = mm(spread[part], heads[k]).astype(BF16)
            value = value + mm(rows, wout[k * DV : (k + 1) * DV, cols])
        pbuf[part] = value.astype(BF16).reshape(4, 32, HALF)

    def scatter(source, landing):
        copies = []
        for part, (fs, es, to_f, to_e) in enumerate(axes):
            for d in (1, 2, 3):
                copies.append(wire.push((source, part, fs[d]), (landing, part, d - 1), to_f[d]))
        return copies

    def summed(first, landing, part):
        value = first.astype(F32)
        for d in range(3):
            value = value + landing[part, d].astype(F32)
        return value

    copies = scatter(pbuf, rxa)
    arrive(copies)
    copies = []
    for part, (fs, es, to_f, to_e) in enumerate(axes):
        ebuf[part] = summed(pbuf[part, fs[0]], rxa, part).astype(BF16)
        for d in (1, 2, 3):
            copies.append(wire.push((ebuf, part), (rxb, part, d - 1), to_e[d]))
    arrive(copies)
    for part in range(2):
        zbuf[part] = summed(ebuf[part], rxb, part).astype(BF16)
    copy = wire.push((zbuf,), (rxc,), far)
    copy.wait_recv()
    copies = []
    for part, (fs, es, to_f, to_e) in enumerate(axes):
        value = (zbuf[part].astype(F32) + rxc[part].astype(F32)).astype(BF16)
        hid[part, fs[0]] = value
        hidf[part] = value.astype(F32).reshape(4, 8, HALF)
        for d in (1, 2, 3):
            ref = (hid, part, fs[0])
            copies.append(wire.push(ref, ref, to_f[d]))
    arrive(copies)

    loads[8].wait()
    loads[9].wait()
    eye = iota((96, 128), 0) == iota((96, 128), 1)
    squares = jnp.zeros((96, 1), F32)
    gate = jnp.zeros((96, 512), F32)
    rise = jnp.zeros((96, 512), F32)
    for part in range(2):
        rows = mm(gathered[part], hid[part].reshape(128, HALF))
        squares = squares + jnp.sum(rows * rows, axis=-1, keepdims=True)
        cols = pl.ds(part * HALF, HALF)
        scaled = (rows * gain_ref[0:1, cols]).astype(BF16)
        gate = gate + mm(scaled, wg[cols, :])
        rise = rise + mm(scaled, wu[cols, :])
    sq[...] = jnp.broadcast_to(
        jnp.sum(jnp.where(eye, squares, 0.0), axis=0, keepdims=True), (8, 128)
    )
    for j in range(4):
        gs[j, :, :128] = gate[:, j * 128 : (j + 1) * 128].astype(BF16)
        gs[j, :, 128:] = rise[:, j * 128 : (j + 1) * 128].astype(BF16)
    copies = []
    for d in (1, 2, 3):
        copies.append(wire.push((sq,), (rxs, d - 1), mates[d]))
        copies.append(wire.push((gs, gs_of[d]), (rxg, d - 1), mates[d]))
    arrive(copies)
    both = gs[g].astype(F32)
    total = sq[0:1, :]
    for d in range(3):
        both = both + rxg[d].astype(F32)
        total = total + rxs[d, 0:1, :]
    total = jnp.sum(jnp.where(eye, total, 0.0), axis=-1, keepdims=True)
    both = both * lax.rsqrt(total * (1.0 / D) + 1e-06)
    gate, rise = both[:, :128], both[:, 128:]
    units[g] = (gate / (1.0 + jnp.exp(-gate)) * rise).astype(BF16)
    copies = [wire.push((units, g), (units, g), mates[d]) for d in (1, 2, 3)]
    arrive(copies)
    loads[10].wait()
    for part in range(2):
        cols = pl.ds(part * HALF, HALF)
        value = jnp.zeros((128, HALF), F32)
        for k in range(4):
            rows = mm(spread[part], units[k]).astype(BF16)
            value = value + mm(rows, wd[k * 128 : (k + 1) * 128, cols])
        value = value.astype(BF16).astype(F32) * fac[part, :, 0:1]
        part_buf[part] = value.astype(BF16).reshape(4, 32, HALF)
    copies = scatter(part_buf, rxq)
    arrive(copies)
    copies = []
    for part, (fs, es, to_f, to_e) in enumerate(axes):
        ybuf[part] = summed(part_buf[part, fs[0]], rxq, part).reshape(4, 8, HALF)
        for d in (1, 2, 3):
            copies.append(wire.push((ybuf, part, es[d]), (rxy, part, d - 1), to_e[d]))
    arrive(copies)
    for part, (fs, es, to_f, to_e) in enumerate(axes):
        wbuf[part] = summed(ybuf[part, es[0]], rxy, part)
    copy = wire.push((wbuf,), (rxw,), far)
    copy.wait_recv()
    for part, (fs, es, to_f, to_e) in enumerate(axes):
        value = hidf[part, es[0]] + (wbuf[part] + rxw[part])
        fo[g, part * 4 : (part + 1) * 4, :] = jnp.where(z == 0, value[0:4], value[4:8])
    copies = [wire.push((fo, g), (fo, g), mates[d]) for d in (1, 2, 3)]
    arrive(copies)
    for k in range(4):
        for part in range(2):
            at_ = k * QUARTER + part * HALF
            out_ref[:, at_ : at_ + HALF] = fo[k, part * 4 : part * 4 + SEQS, :].astype(BF16)
    wire.finish()


def vmem():
    return pl.BlockSpec(memory_space=pltpu.VMEM)


def hbm():
    return pl.BlockSpec(memory_space=pl.ANY)


def on_device(
    queries, cache, value_up_weight, w_out, resid, norm_gain, routes, route_weight,
    w_gate, w_up, w_down,
):
    g, c, x, y, z = place()
    pair, core = lax.rem(g // 2 + z, 2), g % 2
    by_column = queries.reshape(SEQS, 16, 8, QK)
    lower = lax.dynamic_index_in_dim(by_column, 2 * pair + core, 2, keepdims=False)
    upper = lax.dynamic_index_in_dim(by_column, 4 + 2 * (1 - pair) + core, 2, keepdims=False)
    matches = routes[:, 0, :, None] == jnp.arange(EXPERTS, dtype=jnp.int32)
    weights = jnp.sum(
        jnp.where(matches, route_weight[:, 0, :, None].astype(F32), 0.0), axis=1
    ).astype(BF16)
    spare = jnp.pad(weights, ((0, 0), (0, QPAD - QK - EXPERTS)))
    spare = jnp.broadcast_to(spare[:, None, None, :], (SEQS, 2, 16, QPAD - QK))
    rows = jnp.concatenate([jnp.stack([lower, upper], axis=1), spare], axis=-1)

    own_resid = lax.dynamic_slice_in_dim(resid[:, 0], g * QUARTER, QUARTER, 1)
    own_resid = jnp.pad(own_resid, ((0, 16 - SEQS), (0, 0)))
    own_gain = lax.dynamic_slice_in_dim(norm_gain, g * QUARTER, QUARTER, 0)
    own_gain = jnp.broadcast_to(own_gain[None], (8, QUARTER))
    mixed = pl.pallas_call(
        kernel,
        out_shape=jax.ShapeDtypeStruct((SEQS, D), BF16),
        in_specs=[vmem(), hbm(), hbm(), hbm(), vmem(), vmem(), hbm(), hbm(), hbm()],
        out_specs=vmem(),
        scratch_shapes=[
            pltpu.VMEM((SEQS, 4, 4, 2, 2, 16, QPAD), BF16),
            pltpu.VMEM((SEQS, QPAD, CTX_DEV), BF16),
            pltpu.VMEM((256, CTX_DEV), F32),
            pltpu.VMEM((256, CTX_DEV), F32),
            pltpu.VMEM((256, CTX_DEV), BF16),
            pltpu.VMEM((256, CTX_DEV), BF16),
            pltpu.VMEM((2, 5, 256, 128), F32),
            pltpu.VMEM((SEQS, 2, 4, 4, 2, 16, QPAD), BF16),
            pltpu.VMEM((SEQS, 2, 2, 2, 2, 16, QPAD), BF16),
            pltpu.VMEM((SEQS, 2, 2, 4, 2, 16, QPAD), BF16),
            pltpu.VMEM((SEQS, 2, 3, 2, 16, QPAD), BF16),
            pltpu.VMEM((SEQS, 2, 2, 16, QPAD), BF16),
            pltpu.VMEM((SEQS, 2, 16, QPAD), BF16),
            pltpu.VMEM((96, KVL), BF16),
            pltpu.VMEM((2, 128, 128), F32),
            pltpu.VMEM((KVL, DV), BF16),
            pltpu.VMEM((512, QUARTER), BF16),
            pltpu.VMEM((QUARTER, 512), BF16),
            pltpu.VMEM((QUARTER, 512), BF16),
            pltpu.VMEM((512, QUARTER), BF16),
            pltpu.VMEM((4, 96, DV), BF16),
            pltpu.VMEM((2, 4, 32, HALF), BF16),
            pltpu.VMEM((2, 3, 32, HALF), BF16),
            pltpu.VMEM((2, 32, HALF), BF16),
            pltpu.VMEM((2, 3, 32, HALF), BF16),
            pltpu.VMEM((2, 32, HALF), BF16),
            pltpu.VMEM((2, 32, HALF), BF16),
            pltpu.VMEM((2, 4, 32, HALF), BF16),
            pltpu.VMEM((2, 4, 8, HALF), F32),
            pltpu.VMEM((8, 128), F32),
            pltpu.VMEM((3, 8, 128), F32),
            pltpu.VMEM((4, 96, 256), BF16),
            pltpu.VMEM((3, 96, 256), BF16),
            pltpu.VMEM((4, 96, 128), BF16),
            pltpu.VMEM((2, 4, 32, HALF), BF16),
            pltpu.VMEM((2, 3, 32, HALF), BF16),
            pltpu.VMEM((2, 4, 8, HALF), F32),
            pltpu.VMEM((2, 3, 8, HALF), F32),
            pltpu.VMEM((2, 8, HALF), F32),
            pltpu.VMEM((2, 8, HALF), F32),
            pltpu.VMEM((4, 8, HALF), F32),
            pltpu.SemaphoreType.DMA((160,)),
            pltpu.SemaphoreType.DMA((160,)),
            pltpu.SemaphoreType.DMA((11,)),
        ],
        compiler_params=pltpu.CompilerParams(
            collective_id=0, has_side_effects=True, vmem_limit_bytes=60 * 1024 * 1024
        ),
    )(rows, jnp.swapaxes(cache, 1, 2), value_up_weight, w_out, own_resid, own_gain, w_gate, w_up, w_down)
    return mixed.reshape(SEQS, 1, D)


def solution(mesh):
    placed = (
        P(None, "cp", None),
        P(None, "cp", None),
        P("cp", None, None),
        P("cp", None),
        P(None, "cp", None),
        P(),
        P(None, "cp", None),
        P(None, "cp", None),
        P("cp", "grp", None),
        P("cp", "grp", None),
        P("cp", None, "grp"),
    )
    return jax.shard_map(
        on_device, mesh=mesh, in_specs=placed, out_specs=P(None, "cp", None), check_vma=False
    )
```

time: 168 us -> 147 us (0.88)
  local copies, waits for them, and re-layouts: 22.1 us -> 5.46 us
  Pallas kernels: 143 us -> 140 us
    unnamed x19 -> x8, local copies, waits for them, and re-layouts: 19.4 us -> 1.48 us
    pallas_call x2 -> x1, Pallas kernels: 143 us -> 140 us  [on_device(): pl.pallas_call(kernel, out_shape=jax.ShapeDtypeStruct((SEQS, D), BF16), i...]
where the time goes in v2:
time: 147 us
  Pallas kernels  140 us (95%)
  local copies, waits for them, and re-layouts  5.46 us (4%)
    pallas_call x1, Pallas kernels, on_device(): pl.pallas_call(kernel, out_shape=jax.ShapeDtypeStruct((SEQS, D), BF16), i...  140 us

profile of v2, /device:TPU:1, one launch (start us, length us, event | category | flops | bytes accessed | tf_op | source)
XLA Modules:
  0.0 146.7 jit_solution(9960846888160704773)
XLA Ops:
  0.0 0.0 copy-start
  0.0 0.0 copy-start.1
  0.0 0.0 copy-start.2
  0.1 1.6 %reshape.21 = bf16[3,16,8,576]{3,2,1,0:T(8,128)(2,1)S(1)} reshape(bf16[3,1,73728]{2,0,1:T(4,128)(2,1)} %param.11) | data formatting | bytes 884736 | tf_op jit(solution)/shard_map/reshape | solution.py:554
  1.7 0.3 constant_dynamic-slice_fusion.1
  2.0 0.0 copy-done.1
  2.0 0.0 copy-done.2
  2.0 0.1 select_reduce_fusion
  2.1 0.7 pad_maximum_fusion.q_ref
  2.9 0.0 copy-done
  2.9 0.6 pad.9.resid_ref
  3.5 0.8 dynamic_slice.19
  4.3 0.6 broadcast_in_dim.28.gain_ref
  4.9 140.3 %shard_map.109 = bf16[3,7168]{1,0:T(4,128)(2,1)} custom-call(bf16[3,2,16,640]{3,2,1,0:T(8,128)(2,1)} %pad_maximum_fusion.q_ref, bf16[3,576,2048]{2,1,0:T(8,128)(2,1)} %bitcast.16, bf16[4,512,128]{2,1,0:T(8,128)(2,1)} %vup_ref.1, bf16[512,7168]{1,0:T(8,128)(2,1)} %wout_ref.1, bf16[16,1792]{1,0:T(8,128)(2,1)} %pad.9.resid_ref, ...), custom_call_target="tpu_custom_call" | custom-call | tf_op jit(solution)/shard_map/pallas_call | solution.py:569
  145.2 1.5 copy.24
  (6 shorter events, 0.1 us)
Async XLA Ops:
  0.0 2.9 %copy-start = (bf16[3,1,7168]{2,0,1:T(4,128)(2,1)S(1)}, bf16[3,1,7168]{2,0,1:T(4,128)(2,1)}, u32[]{:S(2)}) copy-start(bf16[3,1,7168]{2,0,1:T(4,128)(2,1)} %param.15) | copy-start | bytes 129028
  0.0 2.0 %copy-start.1 = (s32[3,1,4]{2,1,0:T(1,128)S(1)}, s32[3,1,4]{2,1,0:T(1,128)}, u32[]{:S(2)}) copy-start(s32[3,1,4]{2,1,0:T(1,128)} %param.17) | copy-start | bytes 148
  0.0 2.0 %copy-start.2 = (bf16[3,1,4]{2,0,1:T(4,128)(2,1)S(1)}, bf16[3,1,4]{2,0,1:T(4,128)(2,1)}, u32[]{:S(2)}) copy-start(bf16[3,1,4]{2,0,1:T(4,128)(2,1)} %param.18) | copy-start | bytes 76

commit v3 on v2

--- a/solution.py
+++ b/solution.py
@@ -139,14 +139,15 @@
 
 def put(ref, merged):
     out, peak, total = merged
-    ref[..., :KVL] = out.astype(BF16).reshape(2, 16, KVL)
-    ref[..., KVL:] = aux_lanes(peak, total).astype(BF16).reshape(2, 16, QPAD - KVL)
+    ref[..., :KVL] = out.astype(BF16).reshape(*ref.shape[:-1], KVL)
+    ref[..., KVL:] = aux_lanes(peak, total).astype(BF16).reshape(*ref.shape[:-1], QPAD - KVL)
 
 
 def kernel(
-    q_ref, cache_ref, vup_ref, wout_ref, resid_ref, gain_ref, wg_ref, wu_ref, wd_ref, out_ref,
-    qbuf, kv, score_a, score_b, prob_a, prob_b, oscr, msg, rx1, rx2, rx3, fin, rxz, lat, fac,
-    vup, wout, wg, wu, wd, heads, pbuf, rxa, ebuf, rxb, zbuf, rxc, hid, hidf,
+    q_ref, cache_ref, vup_ref, wout_ref, resid_ref, gain_ref, routes_ref, weight_ref,
+    wg_ref, wu_ref, wd_ref, out_ref,
+    qbuf, kv, score_a, score_b, prob_a, prob_b, oscr, msg, rx1, rx2, rx3, fin, rxz, lat,
+    vup, wout, wg, wu, wd, own_resid, heads, pbuf, rxa, ebuf, rxb, zbuf, rxc, hid, hidf,
     sq, rxs, gs, rxg, units, part_buf, rxq, ybuf, rxy, wbuf, rxw, fo,
     send_sems, recv_sems, local_sems,
 ):
@@ -165,7 +166,7 @@
     gs_of = [g] + [up(g, d) for d in (1, 2, 3)]
     mates = [None] + [(gs_of[d], c) for d in (1, 2, 3)]
     columns = pl.ds(pl.multiple_of(g * QUARTER, 128), QUARTER)
-    pairs = [(q_ref.at[s], qbuf.at[s, x, y, z]) for s in range(SEQS)]
+    pairs = [(q_ref, qbuf.at[:, x, y, z])]
     pairs += [(cache_ref.at[s], kv.at[s, pl.ds(0, QK)]) for s in range(SEQS)]
     pairs += [
         (vup_ref.at[g], vup),
@@ -185,54 +186,52 @@
     )
     wire = Wire(send_sems, recv_sems)
 
+    chunks = [(0, 2), (2, 2), (4, 2)]
     dirs = (1, 3)
     other = 1 - z
 
-    def gather_0(s):
-        return [wire.push((q_ref, s), (qbuf, s, x, y, z), partner)]
-
-    def gather_1(s, copies):
+    def gather_0(k, _):
+        span = pl.ds(*chunks[k])
+        return [wire.push((q_ref, span), (qbuf, span, x, y, z), partner)]
+
+    def gather_1(k, copies):
         arrive(copies)
+        span = pl.ds(*chunks[k])
+        copies = []
+        for d in (1, 2, 3):
+            ref = (qbuf, span, x, y, 0)
+            copies.append(wire.push(ref, ref, to_x[d]))
+            ref = (qbuf, span, x, y, 1)
+            copies.append(wire.push(ref, ref, to_y[d]))
+        return copies
+
+    def gather_3(k, copies):
+        arrive(copies)
+        span = pl.ds(*chunks[k])
         copies = []
         for d in dirs:
-            ref = (qbuf, s, x, y, 0)
-            copies.append(wire.push(ref, ref, to_x[d]))
-            ref = (qbuf, s, x, y, 1)
+            ref = (qbuf, span, slice(None), y, 0)
             copies.append(wire.push(ref, ref, to_y[d]))
-        return copies
-
-    def gather_2(s, copies):
-        arrive(copies)
-        copies = []
-        for k, d in enumerate(dirs):
-            ref = (qbuf, s, xs[4 - d], y, 0, k)
-            copies.append(wire.push(ref, ref, to_x[d]))
-            ref = (qbuf, s, x, ys[4 - d], 1, k)
-            copies.append(wire.push(ref, ref, to_y[d]))
-        return copies
-
-    def gather_3(s, copies):
-        arrive(copies)
-        copies = []
-        for d in dirs:
-            ref = (qbuf, s, slice(None), y, 0)
-            copies.append(wire.push(ref, ref, to_y[d]))
-            ref = (qbuf, s, x, slice(None), 1)
+            ref = (qbuf, span, x, slice(None), 1)
             copies.append(wire.push(ref, ref, to_x[d]))
         return copies
 
-    def gather_4(s, copies):
+    def gather_4(k, copies):
         arrive(copies)
+        span = pl.ds(*chunks[k])
         copies = []
-        for k, d in enumerate(dirs):
-            ref = (qbuf, s, pl.ds(2 * k, 2), ys[4 - d], 0)
+        for n, d in enumerate(dirs):
+            ref = (qbuf, span, pl.ds(2 * n, 2), ys[4 - d], 0)
             copies.append(wire.push(ref, ref, to_y[d]))
-            ref = (qbuf, s, xs[4 - d], pl.ds(2 * k, 2), 1)
+            ref = (qbuf, span, xs[4 - d], pl.ds(2 * n, 2), 1)
             copies.append(wire.push(ref, ref, to_x[d]))
         return copies
 
-    def scores(s, half, part, score):
-        q = qbuf[s, 2 * part : 2 * part + 2, :, :, half].reshape(256, QPAD)
+    def gather_5(k, copies):
+        arrive(copies)
+
+    def scores(t, s, part, score):
+        q = qbuf[t, 2 * part : 2 * part + 2].reshape(256, QPAD)
         for n in range(4):
             keys = pl.ds(n * 512, 512)
             value = mm(q, kv[s, :, keys])
@@ -246,7 +245,7 @@
                     position <= CTX - QROWS + row, value[:, 384:], -1e30
                 )
 
-    def weigh(s, half, part, score, prob):
+    def weigh(t, s, part, score, prob):
         peak = jnp.max(score[...], axis=-1, keepdims=True).astype(BF16).astype(F32)
         total = jnp.zeros((256, 128), F32)
         for n in range(4):
@@ -264,150 +263,119 @@
             a, b = (n // 4, n % 4) if part == 0 else (n % 4, n // 4)
             for m in range(5):
                 lanes = pl.ds(m * 128, 128)
-                msg[s, part, a, b, half, :, lanes] = oscr[
+                msg[t, part, a, b, :, lanes] = oscr[
                     part, m, pl.ds(n, 16, stride=16), :
                 ].astype(BF16)
 
     def attend(t):
-        s, half = t // 2, t % 2
-        scores(s, half, 0, score_a)
-        scores(s, half, 1, score_b)
-        weigh(s, half, 0, score_a, prob_a)
-        weigh(s, half, 1, score_b, prob_b)
+        s = t // 2
+        scores(t, s, 0, score_a)
+        scores(t, s, 1, score_b)
+        weigh(t, s, 0, score_a, prob_a)
+        weigh(t, s, 1, score_b, prob_b)
 
     axes = [(xs, ys, to_x, to_y), (ys, xs, to_y, to_x)]
 
-    def reduce_1(s):
+    def reduce_1(k, _):
+        span = pl.ds(*chunks[k])
         copies = []
         for part, (fs, es, to_f, to_e) in enumerate(axes):
-            for k, d in enumerate(dirs):
-                src = (msg, s, part, fs[2], pl.ds(2 * k, 2))
-                copies.append(wire.push(src, (rx1, s, part, k), to_f[d]))
+            for n, d in enumerate(dirs):
+                src = (msg, span, part, fs[2], pl.ds(2 * n, 2))
+                copies.append(wire.push(src, (rx1, span, part, n), to_f[d]))
         return copies
 
-    def reduce_2(s, copies):
+    def reduce_2(k, copies):
         arrive(copies)
+        span = pl.ds(*chunks[k])
         copies = []
         for part, (fs, es, to_f, to_e) in enumerate(axes):
-            for k, d in enumerate(dirs):
-
-                @pl.loop(0, 2)
-                def _(j):
-                    put(
-                        msg.at[s, part, fs[d], 2 * k + j],
-                        merge([msg[s, part, fs[d], 2 * k + j], rx1[s, part, k, j]]),
-                    )
-
-                copies.append(wire.push((msg, s, part, fs[d]), (rx2, s, part, k), to_f[d]))
+            for n, d in enumerate(dirs):
+
+                @pl.loop(chunks[k][0], sum(chunks[k]))
+                def _(t):
+                    ref = msg.at[t, part, fs[d], pl.ds(2 * n, 2)]
+                    put(ref, merge([ref[...], rx1[t, part, n]]))
+
+                copies.append(
+                    wire.push((msg, span, part, fs[d]), (rx2, span, part, n), to_f[d])
+                )
         return copies
 
-    def reduce_3(s, copies):
+    def reduce_3(k, copies):
         arrive(copies)
+        span = pl.ds(*chunks[k])
         copies = []
         for part, (fs, es, to_f, to_e) in enumerate(axes):
 
-            @pl.loop(0, 4)
-            def _(j):
+            @pl.loop(2 * chunks[k][0], 2 * sum(chunks[k]))
+            def _(at_):
+                t, units = at_ // 2, pl.ds(2 * (at_ % 2), 2)
+                ref = msg.at[t, part, fs[0], units]
+                put(ref, merge([ref[...], rx2[t, part, 0, units], rx2[t, part, 1, units]]))
+
+            for d in (1, 2, 3):
+                src = (msg, span, part, fs[0], es[d])
+                copies.append(wire.push(src, (rx3, span, part, d - 1), to_e[d]))
+        return copies
+
+    def reduce_4(k, copies):
+        arrive(copies)
+
+        @pl.loop(chunks[k][0], sum(chunks[k]))
+        def _(t):
+            for part, (fs, es, to_f, to_e) in enumerate(axes):
                 put(
-                    msg.at[s, part, fs[0], j],
-                    merge([msg[s, part, fs[0], j], rx2[s, part, 0, j], rx2[s, part, 1, j]]),
+                    fin.at[t, part],
+                    merge([msg[t, part, fs[0], es[0]]] + [rx3[t, part, d] for d in range(3)]),
                 )
 
-            for d in (1, 2, 3):
-                src = (msg, s, part, fs[0], es[d])
-                copies.append(wire.push(src, (rx3, s, part, d - 1), to_e[d]))
-        return copies
-
-    def reduce_4(s, copies):
-        arrive(copies)
-        for part, (fs, es, to_f, to_e) in enumerate(axes):
-            out, peak, total = merge(
-                [msg[s, part, fs[0], es[0]]] + [rx3[s, part, d] for d in range(3)]
-            )
-            fin[s, :, part, :, :KVL] = out.astype(BF16).reshape(2, 16, KVL)
-            fin[s, :, part, :, KVL:] = aux_lanes(peak, total).astype(BF16).reshape(
-                2, 16, QPAD - KVL
-            )
-        return [wire.push((fin, s, other), (rxz, s), partner)]
-
-    def reduce_5(s, copies):
-        arrive(copies)
-        out, peak, total = merge([fin[s, z], rxz[s]])
-        lat[s * QROWS : (s + 1) * QROWS, :] = (out / total).astype(BF16)
-
-    zs = [gather_0(s) for s in range(SEQS)]
-    for copy in loads[:3]:
+        done = [t // 2 for t in range(chunks[k][0], sum(chunks[k])) if t % 2]
+        return [(s, wire.push((fin, 2 * s + other), (rxz, s), partner)) for s in done]
+
+    def reduce_5(k, copies):
+        for s, copy in copies:
+            copy.wait_recv()
+            out, peak, total = merge([fin[2 * s + z], rxz[s]])
+            lat[s * QROWS : (s + 1) * QROWS, :] = (out / total).astype(BF16)
+
+    state = [None] * len(chunks)
+
+    def run(steps):
+        for step, k in steps:
+            state[k] = step(k, state[k])
+
+    loads[0].wait()
+    run([(gather_0, 0)])
+    kv[:, QK:, :] = jnp.zeros((SEQS, QPAD - QK, CTX_DEV), BF16)
+    run([(gather_1, 0), (gather_0, 1), (gather_3, 0), (gather_1, 1), (gather_0, 2)])
+    run([(gather_1, 2), (gather_4, 0), (gather_3, 1), (gather_3, 2)])
+    for copy in loads[1:4]:
         copy.wait()
-    got = [None] * SEQS
-    got[0] = gather_1(0, zs[0])
-    kv[:, QK:, :] = jnp.zeros((SEQS, QPAD - QK, CTX_DEV), BF16)
-    got[0] = gather_2(0, got[0])
-    got[0] = gather_3(0, got[0])
-    got[1] = gather_1(1, zs[1])
-    got[0] = gather_4(0, got[0])
-    got[1] = gather_2(1, got[1])
-    for copy in loads[3:6]:
-        copy.wait()
-    arrive(got[0])
-    got[1] = gather_3(1, got[1])
-    red = [None] * SEQS
+    run([(gather_5, 0)])
+    between = {
+        1: [(gather_4, 1)],
+        2: [(gather_4, 2), (reduce_1, 0), (gather_5, 1)],
+        3: [],
+        4: [(gather_5, 2), (reduce_1, 1), (reduce_2, 0)],
+        5: [(reduce_2, 1)],
+    }
 
     @pl.loop(0, 6)
     def _(t):
-        @pl.when(t == 1)
-        def _():
-            got[1] = gather_4(1, got[1])
-            got[2] = gather_1(2, zs[2])
-            got[2] = gather_2(2, got[2])
-
-        @pl.when(t == 2)
-        def _():
-            arrive(got[1])
-            got[2] = gather_3(2, got[2])
-            red[0] = reduce_1(0)
-
-        @pl.when(t == 3)
-        def _():
-            got[2] = gather_4(2, got[2])
-            red[0] = reduce_2(0, red[0])
-
-        @pl.when(t == 4)
-        def _():
-            arrive(got[2])
-            red[0] = reduce_3(0, red[0])
-            red[1] = reduce_1(1)
-
-        @pl.when(t == 5)
-        def _():
-            red[0] = reduce_4(0, red[0])
-            red[1] = reduce_2(1, red[1])
+        for at_, steps in between.items():
+            if steps:
+
+                @pl.when(t == at_)
+                def _():
+                    run(steps)
 
         attend(t)
 
-    red[2] = reduce_1(2)
-    red[1] = reduce_3(1, red[1])
-    red[2] = reduce_2(2, red[2])
-    red[1] = reduce_4(1, red[1])
-    red[2] = reduce_3(2, red[2])
-
-    for part in range(2):
-        picked = jnp.zeros((128, 128), F32)
-        for s in range(SEQS):
-            seq, row = padded_row((128, 512), 0, part)
-            j = iota((128, 512), 1)
-            pick = ((seq == s) & (j == row * 16)).astype(F32).astype(BF16)
-            picked = picked + mm(pick, qbuf[s, :, :, :, 0, :, KVL:].reshape(512, 128))
-        lane = iota((128, 128), 1)
-        chosen = jnp.sum(
-            jnp.where(lane == QK - KVL + c // SPLIT, picked, 0.0), axis=-1, keepdims=True
-        )
-        fac[part] = jnp.broadcast_to(chosen, (128, 128))
-
-    red[2] = reduce_4(2, red[2])
-    for s in range(SEQS):
-        reduce_5(s, red[s])
-
-    loads[6].wait()
+    run([(reduce_1, 2), (reduce_3, 0), (reduce_3, 1), (reduce_2, 2), (reduce_4, 0), (reduce_4, 1)])
+    run([(reduce_5, 0), (reduce_3, 2), (reduce_5, 1), (reduce_4, 2), (reduce_5, 2)])
+
+    loads[4].wait()
     heads[g] = mm(lat[...], vup[...]).astype(BF16)
     copies = [wire.push((heads, g), (heads, g), mates[d]) for d in (1, 2, 3)]
     spread, gathered = [], []
@@ -423,16 +391,28 @@
             ((seq < SEQS) & (j == seq * QROWS + row)).astype(F32).astype(BF16)
         )
     arrive(copies)
-    loads[7].wait()
+    loads[5].wait()
+    own_resid[...] = jnp.zeros((16, QUARTER), BF16)
+    own_resid[0:SEQS, :] = resid_ref[0, :, columns]
+    lane = iota((1, 128), 1)
+    gates = jnp.zeros((1, 128), F32)
+    for s in range(SEQS):
+        for r in range(4):
+            here = lane == s * EXPERTS + routes_ref[s, :, r : r + 1]
+            gates = gates + jnp.where(here, weight_ref[0, s : s + 1, r : r + 1].astype(F32), 0.0)
     for part in range(2):
         cols = pl.ds(part * HALF, HALF)
         seq, row = padded_row((128, 16), 0, part)
         mine = ((row == c) & (seq == iota((128, 16), 1)) & (seq < SEQS)).astype(F32).astype(BF16)
-        value = mm(mine, resid_ref[:, cols])
+        value = mm(mine, own_resid[:, cols])
         for k in range(4):
             rows = mm(spread[part], heads[k]).astype(BF16)
             value = value + mm(rows, wout[k * DV : (k + 1) * DV, cols])
         pbuf[part] = value.astype(BF16).reshape(4, 32, HALF)
+        if part == 0:
+            seq, row = padded_row((128, 128), 0, part)
+            head = jnp.where((seq == SEQS) & (row == c), gates, value[:, :128])
+            pbuf[part, :, :, :128] = head.astype(BF16).reshape(4, 32, 128)
 
     def scatter(source, landing):
         copies = []
@@ -469,8 +449,8 @@
             copies.append(wire.push(ref, ref, to_f[d]))
     arrive(copies)
 
-    loads[8].wait()
-    loads[9].wait()
+    loads[6].wait()
+    loads[7].wait()
     eye = iota((96, 128), 0) == iota((96, 128), 1)
     squares = jnp.zeros((96, 1), F32)
     gate = jnp.zeros((96, 512), F32)
@@ -479,7 +459,13 @@
         rows = mm(gathered[part], hid[part].reshape(128, HALF))
         squares = squares + jnp.sum(rows * rows, axis=-1, keepdims=True)
         cols = pl.ds(part * HALF, HALF)
-        scaled = (rows * gain_ref[0:1, cols]).astype(BF16)
+        scaled = jnp.concatenate(
+            [
+                rows[:, n * 128 : (n + 1) * 128] * gain_ref[pl.ds(g * 14 + part * 7 + n, 1), :]
+                for n in range(7)
+            ],
+            axis=1,
+        ).astype(BF16)
         gate = gate + mm(scaled, wg[cols, :])
         rise = rise + mm(scaled, wu[cols, :])
     sq[...] = jnp.broadcast_to(
@@ -492,6 +478,15 @@
     for d in (1, 2, 3):
         copies.append(wire.push((sq,), (rxs, d - 1), mates[d]))
         copies.append(wire.push((gs, gs_of[d]), (rxg, d - 1), mates[d]))
+    table = hid[0, :, :, :128].reshape(128, 128)
+    factors = []
+    for part in range(2):
+        seq, row = padded_row((128, 128), 0, part)
+        pick = (iota((128, 128), 1) == row * 4 + SEQS).astype(F32).astype(BF16)
+        here = iota((128, 128), 1) == seq * EXPERTS + c // SPLIT
+        factors.append(
+            jnp.sum(jnp.where(here, mm(pick, table), 0.0), axis=-1, keepdims=True)
+        )
     arrive(copies)
     both = gs[g].astype(F32)
     total = sq[0:1, :]
@@ -504,14 +499,14 @@
     units[g] = (gate / (1.0 + jnp.exp(-gate)) * rise).astype(BF16)
     copies = [wire.push((units, g), (units, g), mates[d]) for d in (1, 2, 3)]
     arrive(copies)
-    loads[10].wait()
+    loads[8].wait()
     for part in range(2):
         cols = pl.ds(part * HALF, HALF)
         value = jnp.zeros((128, HALF), F32)
         for k in range(4):
             rows = mm(spread[part], units[k]).astype(BF16)
             value = value + mm(rows, wd[k * 128 : (k + 1) * 128, cols])
-        value = value.astype(BF16).astype(F32) * fac[part, :, 0:1]
+        value = value.astype(BF16).astype(F32) * factors[part]
         part_buf[part] = value.astype(BF16).reshape(4, 32, HALF)
     copies = scatter(part_buf, rxq)
     arrive(copies)
@@ -554,44 +549,34 @@
     by_column = queries.reshape(SEQS, 16, 8, QK)
     lower = lax.dynamic_index_in_dim(by_column, 2 * pair + core, 2, keepdims=False)
     upper = lax.dynamic_index_in_dim(by_column, 4 + 2 * (1 - pair) + core, 2, keepdims=False)
-    matches = routes[:, 0, :, None] == jnp.arange(EXPERTS, dtype=jnp.int32)
-    weights = jnp.sum(
-        jnp.where(matches, route_weight[:, 0, :, None].astype(F32), 0.0), axis=1
-    ).astype(BF16)
-    spare = jnp.pad(weights, ((0, 0), (0, QPAD - QK - EXPERTS)))
-    spare = jnp.broadcast_to(spare[:, None, None, :], (SEQS, 2, 16, QPAD - QK))
-    rows = jnp.concatenate([jnp.stack([lower, upper], axis=1), spare], axis=-1)
-
-    own_resid = lax.dynamic_slice_in_dim(resid[:, 0], g * QUARTER, QUARTER, 1)
-    own_resid = jnp.pad(own_resid, ((0, 16 - SEQS), (0, 0)))
-    own_gain = lax.dynamic_slice_in_dim(norm_gain, g * QUARTER, QUARTER, 0)
-    own_gain = jnp.broadcast_to(own_gain[None], (8, QUARTER))
+    rows = jnp.stack([lower, upper], axis=1).reshape(2 * SEQS, 16, QK)
+    rows = jnp.pad(rows, ((0, 0), (0, 0), (0, QPAD - QK)))
     mixed = pl.pallas_call(
         kernel,
         out_shape=jax.ShapeDtypeStruct((SEQS, D), BF16),
-        in_specs=[vmem(), hbm(), hbm(), hbm(), vmem(), vmem(), hbm(), hbm(), hbm()],
+        in_specs=[vmem(), hbm(), hbm(), hbm(), vmem(), vmem(), vmem(), vmem(), hbm(), hbm(), hbm()],
         out_specs=vmem(),
         scratch_shapes=[
-            pltpu.VMEM((SEQS, 4, 4, 2, 2, 16, QPAD), BF16),
+            pltpu.VMEM((6, 4, 4, 2, 16, QPAD), BF16),
             pltpu.VMEM((SEQS, QPAD, CTX_DEV), BF16),
             pltpu.VMEM((256, CTX_DEV), F32),
             pltpu.VMEM((256, CTX_DEV), F32),
             pltpu.VMEM((256, CTX_DEV), BF16),
             pltpu.VMEM((256, CTX_DEV), BF16),
             pltpu.VMEM((2, 5, 256, 128), F32),
-            pltpu.VMEM((SEQS, 2, 4, 4, 2, 16, QPAD), BF16),
-            pltpu.VMEM((SEQS, 2, 2, 2, 2, 16, QPAD), BF16),
-            pltpu.VMEM((SEQS, 2, 2, 4, 2, 16, QPAD), BF16),
-            pltpu.VMEM((SEQS, 2, 3, 2, 16, QPAD), BF16),
-            pltpu.VMEM((SEQS, 2, 2, 16, QPAD), BF16),
+            pltpu.VMEM((6, 2, 4, 4, 16, QPAD), BF16),
+            pltpu.VMEM((6, 2, 2, 2, 16, QPAD), BF16),
+            pltpu.VMEM((6, 2, 2, 4, 16, QPAD), BF16),
+            pltpu.VMEM((6, 2, 3, 16, QPAD), BF16),
+            pltpu.VMEM((6, 2, 16, QPAD), BF16),
             pltpu.VMEM((SEQS, 2, 16, QPAD), BF16),
             pltpu.VMEM((96, KVL), BF16),
-            pltpu.VMEM((2, 128, 128), F32),
             pltpu.VMEM((KVL, DV), BF16),
             pltpu.VMEM((512, QUARTER), BF16),
             pltpu.VMEM((QUARTER, 512), BF16),
             pltpu.VMEM((QUARTER, 512), BF16),
             pltpu.VMEM((512, QUARTER), BF16),
+            pltpu.VMEM((16, QUARTER), BF16),
             pltpu.VMEM((4, 96, DV), BF16),
             pltpu.VMEM((2, 4, 32, HALF), BF16),
             pltpu.VMEM((2, 3, 32, HALF), BF16),
@@ -620,7 +605,19 @@
         compiler_params=pltpu.CompilerParams(
             collective_id=0, has_side_effects=True, vmem_limit_bytes=60 * 1024 * 1024
         ),
-    )(rows, jnp.swapaxes(cache, 1, 2), value_up_weight, w_out, own_resid, own_gain, w_gate, w_up, w_down)
+    )(
+        rows,
+        jnp.swapaxes(cache, 1, 2),
+        value_up_weight,
+        w_out,
+        jnp.swapaxes(resid, 0, 1),
+        norm_gain.reshape(D // 128, 128),
+        routes,
+        jnp.swapaxes(route_weight, 0, 1),
+        w_gate,
+        w_up,
+        w_down,
+    )
     return mixed.reshape(SEQS, 1, D)
 
 

time: 147 us -> 131 us (0.89)
  Pallas kernels: 140 us -> 127 us
    pallas_call x1, Pallas kernels: 140 us -> 127 us  [on_device(): pl.pallas_call(kernel, out_shape=jax.ShapeDtypeStruct((SEQS, D), BF16), i...]
where the time goes in v3:
time: 131 us
  Pallas kernels  127 us (97%)
  local copies, waits for them, and re-layouts  4.03 us (3%)
    pallas_call x1, Pallas kernels, on_device(): pl.pallas_call(kernel, out_shape=jax.ShapeDtypeStruct((SEQS, D), BF16), i...  127 us

profile of v3, /device:TPU:1, one launch (start us, length us, event | category | flops | bytes accessed | tf_op | source)
XLA Modules:
  0.0 130.9 jit_solution(14445679392876563086)
XLA Ops:
  0.0 1.6 %reshape.14 = bf16[3,16,8,576]{3,2,1,0:T(8,128)(2,1)S(1)} reshape(bf16[3,1,73728]{2,0,1:T(4,128)(2,1)} %param.11) | data formatting | bytes 884736 | tf_op jit(solution)/shard_map/reshape | solution.py:549
  1.6 0.3 constant_dynamic-slice_fusion.1
  2.0 0.7 pad.4.q_ref
  2.6 126.8 %shard_map.109 = bf16[3,7168]{1,0:T(4,128)(2,1)} custom-call(bf16[6,16,640]{2,1,0:T(8,128)(2,1)} %pad.4.q_ref, bf16[3,576,2048]{2,1,0:T(8,128)(2,1)} %bitcast.12, bf16[4,512,128]{2,1,0:T(8,128)(2,1)} %vup_ref.1, bf16[512,7168]{1,0:T(8,128)(2,1)} %wout_ref.1, bf16[1,3,7168]{2,1,0:T(4,128)(2,1)} %bitcast.15, f32[56,128]{1,0:T(8,128)} %bitcast.16, ...), custom_call_target="tpu_custom_call" | custom-call | tf_op jit(solution)/shard_map/pallas_call | solution.py:554
  129.5 1.5 %copy.19 = bf16[3,1,7168]{2,0,1:T(4,128)(2,1)} copy(bf16[3,1,7168]{2,0,1:T(4,128)(2,1)} %bitcast.14) | data formatting | bytes 86016
  (3 shorter events, 0.1 us)

commit v4 on v3

--- a/solution.py
+++ b/solution.py
@@ -186,7 +186,7 @@
     )
     wire = Wire(send_sems, recv_sems)
 
-    chunks = [(0, 2), (2, 2), (4, 2)]
+    chunks = [(0, 1), (1, 1), (2, 1), (3, 1), (4, 1), (5, 1)]
     dirs = (1, 3)
     other = 1 - z
 
@@ -346,19 +346,49 @@
             state[k] = step(k, state[k])
 
     loads[0].wait()
-    run([(gather_0, 0)])
+    run([(gather_0, 0), (gather_0, 1)])
     kv[:, QK:, :] = jnp.zeros((SEQS, QPAD - QK, CTX_DEV), BF16)
-    run([(gather_1, 0), (gather_0, 1), (gather_3, 0), (gather_1, 1), (gather_0, 2)])
-    run([(gather_1, 2), (gather_4, 0), (gather_3, 1), (gather_3, 2)])
+    run([(gather_1, 0), (gather_0, 2), (gather_1, 1)])
+    run([(gather_3, 0), (gather_0, 3), (gather_1, 2)])
+    run([(gather_3, 1), (gather_0, 4), (gather_1, 3)])
+    run([(gather_4, 0), (gather_0, 5), (gather_3, 2)])
+    run([(gather_1, 4), (gather_4, 1), (gather_1, 5)])
+    run([(gather_3, 3)])
     for copy in loads[1:4]:
         copy.wait()
     run([(gather_5, 0)])
     between = {
-        1: [(gather_4, 1)],
-        2: [(gather_4, 2), (reduce_1, 0), (gather_5, 1)],
-        3: [],
-        4: [(gather_5, 2), (reduce_1, 1), (reduce_2, 0)],
-        5: [(reduce_2, 1)],
+        1: [
+            (gather_4, 2),
+            (reduce_1, 0),
+            (gather_5, 1),
+            (gather_3, 4),
+        ],
+        2: [
+            (gather_4, 3),
+            (gather_5, 2),
+            (gather_3, 5),
+            (reduce_1, 1),
+        ],
+        3: [
+            (reduce_1, 2),
+            (gather_4, 4),
+            (reduce_2, 0),
+            (gather_5, 3),
+        ],
+        4: [
+            (reduce_2, 1),
+            (gather_4, 5),
+            (reduce_1, 3),
+            (reduce_2, 2),
+            (gather_5, 4),
+        ],
+        5: [
+            (reduce_3, 0),
+            (reduce_3, 1),
+            (gather_5, 5),
+            (reduce_1, 4),
+        ],
     }
 
     @pl.loop(0, 6)
@@ -372,8 +402,13 @@
 
         attend(t)
 
-    run([(reduce_1, 2), (reduce_3, 0), (reduce_3, 1), (reduce_2, 2), (reduce_4, 0), (reduce_4, 1)])
-    run([(reduce_5, 0), (reduce_3, 2), (reduce_5, 1), (reduce_4, 2), (reduce_5, 2)])
+    run([(reduce_1, 5), (reduce_4, 0), (reduce_3, 2)])
+    run([(reduce_4, 1), (reduce_2, 3), (reduce_2, 4)])
+    run([(reduce_5, 0), (reduce_2, 5), (reduce_5, 1)])
+    run([(reduce_4, 2), (reduce_3, 3), (reduce_5, 2)])
+    run([(reduce_3, 4), (reduce_3, 5), (reduce_4, 3)])
+    run([(reduce_4, 4), (reduce_4, 5), (reduce_5, 3)])
+    run([(reduce_5, 4), (reduce_5, 5)])
 
     loads[4].wait()
     heads[g] = mm(lat[...], vup[...]).astype(BF16)
@@ -598,8 +633,8 @@
             pltpu.VMEM((2, 8, HALF), F32),
             pltpu.VMEM((2, 8, HALF), F32),
             pltpu.VMEM((4, 8, HALF), F32),
-            pltpu.SemaphoreType.DMA((160,)),
-            pltpu.SemaphoreType.DMA((160,)),
+            pltpu.SemaphoreType.DMA((240,)),
+            pltpu.SemaphoreType.DMA((240,)),
             pltpu.SemaphoreType.DMA((11,)),
         ],
         compiler_params=pltpu.CompilerParams(

time: 131 us -> 126 us (0.962)
  Pallas kernels: 127 us -> 121 us
    pallas_call x1, Pallas kernels: 127 us -> 121 us  [on_device(): pl.pallas_call(kernel, out_shape=jax.ShapeDtypeStruct((SEQS, D), BF16), i...]
where the time goes in v4:
time: 126 us; the launch traced here: 125 us
  Pallas kernels  121 us (96%)
  local copies, waits for them, and re-layouts  4.03 us (3%)
    pallas_call x1, Pallas kernels, on_device(): pl.pallas_call(kernel, out_shape=jax.ShapeDtypeStruct((SEQS, D), BF16), i...  121 us

profile of v4, /device:TPU:1, one launch (start us, length us, event | category | flops | bytes accessed | tf_op | source)
XLA Modules:
  0.0 125.4 jit_solution(10553314511498463976)
XLA Ops:
  0.0 1.6 %reshape.14 = bf16[3,16,8,576]{3,2,1,0:T(8,128)(2,1)S(1)} reshape(bf16[3,1,73728]{2,0,1:T(4,128)(2,1)} %param.11) | data formatting | bytes 884736 | tf_op jit(solution)/shard_map/reshape | solution.py:584
  1.6 0.3 constant_dynamic-slice_fusion.1
  2.0 0.7 pad.4.q_ref
  2.6 121.3 %shard_map.109 = bf16[3,7168]{1,0:T(4,128)(2,1)} custom-call(bf16[6,16,640]{2,1,0:T(8,128)(2,1)} %pad.4.q_ref, bf16[3,576,2048]{2,1,0:T(8,128)(2,1)} %bitcast.12, bf16[4,512,128]{2,1,0:T(8,128)(2,1)} %vup_ref.1, bf16[512,7168]{1,0:T(8,128)(2,1)} %wout_ref.1, bf16[1,3,7168]{2,1,0:T(4,128)(2,1)} %bitcast.15, f32[56,128]{1,0:T(8,128)} %bitcast.16, ...), custom_call_target="tpu_custom_call" | custom-call | tf_op jit(solution)/shard_map/pallas_call | solution.py:589
  123.9 1.5 %copy.19 = bf16[3,1,7168]{2,0,1:T(4,128)(2,1)} copy(bf16[3,1,7168]{2,0,1:T(4,128)(2,1)} %bitcast.14) | data formatting | bytes 86016
  (3 shorter events, 0.1 us)

commit v5 on v4

--- a/solution.py
+++ b/solution.py
@@ -90,6 +90,16 @@
         copy.wait_recv()
 
 
+def fold(value):
+    rest = jnp.concatenate([value[:, 512:], jnp.zeros((8, 128), value.dtype)], axis=1)
+    return jnp.concatenate([value[:, :512], rest], axis=0).astype(BF16)
+
+
+def unfold(value):
+    value = value.astype(F32)
+    return jnp.concatenate([value[:8], value[8:, : HALF - 512]], axis=1)
+
+
 def greet(peers):
     barrier = pltpu.get_barrier_semaphore()
     for peer in peers:
@@ -147,8 +157,8 @@
     q_ref, cache_ref, vup_ref, wout_ref, resid_ref, gain_ref, routes_ref, weight_ref,
     wg_ref, wu_ref, wd_ref, out_ref,
     qbuf, kv, score_a, score_b, prob_a, prob_b, oscr, msg, rx1, rx2, rx3, fin, rxz, lat,
-    vup, wout, wg, wu, wd, own_resid, heads, pbuf, rxa, ebuf, rxb, zbuf, rxc, hid, hidf,
-    sq, rxs, gs, rxg, units, part_buf, rxq, ybuf, rxy, wbuf, rxw, fo,
+    vup, wout, wg, wu, wd, own_resid, heads, pbuf, rxa, ebuf, rxb, zbuf, hid, hidf,
+    sq, rxs, gs, rxg, units, part_buf, rxq, ybuf, rxy, wbuf, gone, fo,
     send_sems, recv_sems, local_sems,
 ):
     g, c, x, y, z = place()
@@ -163,11 +173,14 @@
     to_y = [None] + [at(x, ys[d], z) for d in (1, 2, 3)]
     partner = (lax.rem(g + 2, 4), (x * 4 + y) * 2 + (1 - z))
     far = at(x, y, 1 - z)
+    far_x = [None] + [at(xs[d], y, 1 - z) for d in (1, 2, 3)]
+    far_y = [None] + [at(x, ys[d], 1 - z) for d in (1, 2, 3)]
     gs_of = [g] + [up(g, d) for d in (1, 2, 3)]
     mates = [None] + [(gs_of[d], c) for d in (1, 2, 3)]
+    far_mates = [(gs_of[d], (x * 4 + y) * 2 + (1 - z)) for d in range(4)]
     columns = pl.ds(pl.multiple_of(g * QUARTER, 128), QUARTER)
     pairs = [(q_ref, qbuf.at[:, x, y, z])]
-    pairs += [(cache_ref.at[s], kv.at[s, pl.ds(0, QK)]) for s in range(SEQS)]
+    pairs += [(cache_ref.at[s], kv.at[s]) for s in range(SEQS)]
     pairs += [
         (vup_ref.at[g], vup),
         (wout_ref.at[:, columns], wout),
@@ -182,7 +195,7 @@
         copy.start()
 
     greet(
-        to_x[1:] + to_y[1:] + mates[1:] + [partner, far]
+        to_x[1:] + to_y[1:] + mates[1:] + far_x[1:] + far_y[1:] + far_mates
     )
     wire = Wire(send_sems, recv_sems)
 
@@ -231,7 +244,7 @@
         arrive(copies)
 
     def scores(t, s, part, score):
-        q = qbuf[t, 2 * part : 2 * part + 2].reshape(256, QPAD)
+        q = qbuf[t, 2 * part : 2 * part + 2].reshape(256, QK)
         for n in range(4):
             keys = pl.ds(n * 512, 512)
             value = mm(q, kv[s, :, keys])
@@ -275,6 +288,7 @@
         weigh(t, s, 1, score_b, prob_b)
 
     axes = [(xs, ys, to_x, to_y), (ys, xs, to_y, to_x)]
+    far_e = [far_y, far_x]
 
     def reduce_1(k, _):
         span = pl.ds(*chunks[k])
@@ -347,7 +361,6 @@
 
     loads[0].wait()
     run([(gather_0, 0), (gather_0, 1)])
-    kv[:, QK:, :] = jnp.zeros((SEQS, QPAD - QK, CTX_DEV), BF16)
     run([(gather_1, 0), (gather_0, 2), (gather_1, 1)])
     run([(gather_3, 0), (gather_0, 3), (gather_1, 2)])
     run([(gather_3, 1), (gather_0, 4), (gather_1, 3)])
@@ -466,19 +479,26 @@
     arrive(copies)
     copies = []
     for part, (fs, es, to_f, to_e) in enumerate(axes):
-        ebuf[part] = summed(pbuf[part, fs[0]], rxa, part).astype(BF16)
+        value = summed(pbuf[part, fs[0]], rxa, part)
+        for k in range(4):
+            ebuf[part, k] = fold(value[k * 8 : (k + 1) * 8])
         for d in (1, 2, 3):
-            copies.append(wire.push((ebuf, part), (rxb, part, d - 1), to_e[d]))
-    arrive(copies)
-    for part in range(2):
-        zbuf[part] = summed(ebuf[part], rxb, part).astype(BF16)
-    copy = wire.push((zbuf,), (rxc,), far)
-    copy.wait_recv()
+            copies.append(wire.push((ebuf, part, es[d]), (rxb, part, d - 1), to_e[d]))
+    arrive(copies)
     copies = []
     for part, (fs, es, to_f, to_e) in enumerate(axes):
-        value = (zbuf[part].astype(F32) + rxc[part].astype(F32)).astype(BF16)
-        hid[part, fs[0]] = value
-        hidf[part] = value.astype(F32).reshape(4, 8, HALF)
+        zbuf[part, z, es[0]] = summed(ebuf[part, es[0]], rxb, part).astype(BF16)
+        ref = (zbuf, part, z, es[0])
+        for peer in [far] + to_e[1:] + far_e[part][1:]:
+            copies.append(wire.push(ref, ref, peer))
+    arrive(copies)
+    copies = []
+    for part, (fs, es, to_f, to_e) in enumerate(axes):
+        for k in range(4):
+            hidf[part, k] = (
+                (unfold(zbuf[part, 0, k]) + unfold(zbuf[part, 1, k])).astype(BF16).astype(F32)
+            )
+        hid[part, fs[0]] = hidf[part].reshape(32, HALF).astype(BF16)
         for d in (1, 2, 3):
             ref = (hid, part, fs[0])
             copies.append(wire.push(ref, ref, to_f[d]))
@@ -553,17 +573,18 @@
     arrive(copies)
     for part, (fs, es, to_f, to_e) in enumerate(axes):
         wbuf[part] = summed(ybuf[part, es[0]], rxy, part)
-    copy = wire.push((wbuf,), (rxw,), far)
-    copy.wait_recv()
     for part, (fs, es, to_f, to_e) in enumerate(axes):
-        value = hidf[part, es[0]] + (wbuf[part] + rxw[part])
-        fo[g, part * 4 : (part + 1) * 4, :] = jnp.where(z == 0, value[0:4], value[4:8])
-    copies = [wire.push((fo, g), (fo, g), mates[d]) for d in (1, 2, 3)]
+        value, whole = wbuf[part], hidf[part, es[0]] + wbuf[part]
+        fo[0, g, part * 4 : (part + 1) * 4, :] = jnp.where(z == 0, whole[0:4], whole[4:8])
+        gone[part * 4 : (part + 1) * 4, :] = jnp.where(z == 0, value[4:8], value[0:4])
+    copies = [wire.push((gone,), (fo, 1, g), far_mates[d]) for d in range(4)]
+    copies += [wire.push((fo, 0, g), (fo, 0, g), mates[d]) for d in (1, 2, 3)]
     arrive(copies)
     for k in range(4):
+        both = fo[0, k] + fo[1, k]
         for part in range(2):
             at_ = k * QUARTER + part * HALF
-            out_ref[:, at_ : at_ + HALF] = fo[k, part * 4 : part * 4 + SEQS, :].astype(BF16)
+            out_ref[:, at_ : at_ + HALF] = both[part * 4 : part * 4 + SEQS].astype(BF16)
     wire.finish()
 
 
@@ -585,15 +606,14 @@
     lower = lax.dynamic_index_in_dim(by_column, 2 * pair + core, 2, keepdims=False)
     upper = lax.dynamic_index_in_dim(by_column, 4 + 2 * (1 - pair) + core, 2, keepdims=False)
     rows = jnp.stack([lower, upper], axis=1).reshape(2 * SEQS, 16, QK)
-    rows = jnp.pad(rows, ((0, 0), (0, 0), (0, QPAD - QK)))
     mixed = pl.pallas_call(
         kernel,
         out_shape=jax.ShapeDtypeStruct((SEQS, D), BF16),
         in_specs=[vmem(), hbm(), hbm(), hbm(), vmem(), vmem(), vmem(), vmem(), hbm(), hbm(), hbm()],
         out_specs=vmem(),
         scratch_shapes=[
-            pltpu.VMEM((6, 4, 4, 2, 16, QPAD), BF16),
-            pltpu.VMEM((SEQS, QPAD, CTX_DEV), BF16),
+            pltpu.VMEM((6, 4, 4, 2, 16, QK), BF16),
+            pltpu.VMEM((SEQS, QK, CTX_DEV), BF16),
             pltpu.VMEM((256, CTX_DEV), F32),
             pltpu.VMEM((256, CTX_DEV), F32),
             pltpu.VMEM((256, CTX_DEV), BF16),
@@ -615,10 +635,9 @@
             pltpu.VMEM((4, 96, DV), BF16),
             pltpu.VMEM((2, 4, 32, HALF), BF16),
             pltpu.VMEM((2, 3, 32, HALF), BF16),
-            pltpu.VMEM((2, 32, HALF), BF16),
-            pltpu.VMEM((2, 3, 32, HALF), BF16),
-            pltpu.VMEM((2, 32, HALF), BF16),
-            pltpu.VMEM((2, 32, HALF), BF16),
+            pltpu.VMEM((2, 4, 16, 512), BF16),
+            pltpu.VMEM((2, 3, 16, 512), BF16),
+            pltpu.VMEM((2, 2, 4, 16, 512), BF16),
             pltpu.VMEM((2, 4, 32, HALF), BF16),
             pltpu.VMEM((2, 4, 8, HALF), F32),
             pltpu.VMEM((8, 128), F32),
@@ -631,10 +650,10 @@
             pltpu.VMEM((2, 4, 8, HALF), F32),
             pltpu.VMEM((2, 3, 8, HALF), F32),
             pltpu.VMEM((2, 8, HALF), F32),
-            pltpu.VMEM((2, 8, HALF), F32),
-            pltpu.VMEM((4, 8, HALF), F32),
-            pltpu.SemaphoreType.DMA((240,)),
-            pltpu.SemaphoreType.DMA((240,)),
+            pltpu.VMEM((8, HALF), F32),
+            pltpu.VMEM((2, 4, 8, HALF), F32),
+            pltpu.SemaphoreType.DMA((250,)),
+            pltpu.SemaphoreType.DMA((250,)),
             pltpu.SemaphoreType.DMA((11,)),
         ],
         compiler_params=pltpu.CompilerParams(

time: 126 us -> 123 us (0.976)
  Pallas kernels: 121 us -> 119 us
    pallas_call x1, Pallas kernels: 121 us -> 119 us  [on_device(): pl.pallas_call(kernel, out_shape=jax.ShapeDtypeStruct((SEQS, D), BF16), i...]
where the time goes in v5:
time: 123 us
  Pallas kernels  119 us (97%)
  local copies, waits for them, and re-layouts  4.02 us (3%)
    pallas_call x1, Pallas kernels, on_device(): pl.pallas_call(kernel, out_shape=jax.ShapeDtypeStruct((SEQS, D), BF16), i...  119 us

profile of v5, /device:TPU:1, one launch (start us, length us, event | category | flops | bytes accessed | tf_op | source)
XLA Modules:
  0.0 122.9 jit_solution(8807473680829807712)
XLA Ops:
  0.0 1.6 %reshape.14 = bf16[3,16,8,576]{3,2,1,0:T(8,128)(2,1)S(1)} reshape(bf16[3,1,73728]{2,0,1:T(4,128)(2,1)} %param.11) | data formatting | bytes 884736 | tf_op jit(solution)/shard_map/reshape | solution.py:605
  1.6 0.3 constant_dynamic-slice_fusion.1
  2.0 0.6 copy.13
  2.6 118.8 %shard_map.109 = bf16[3,7168]{1,0:T(4,128)(2,1)} custom-call(bf16[6,16,576]{2,1,0:T(8,128)(2,1)} %bitcast.13, bf16[3,576,2048]{2,1,0:T(8,128)(2,1)} %bitcast.12, bf16[4,512,128]{2,1,0:T(8,128)(2,1)} %vup_ref.1, bf16[512,7168]{1,0:T(8,128)(2,1)} %wout_ref.1, bf16[1,3,7168]{2,1,0:T(4,128)(2,1)} %bitcast.15, f32[56,128]{1,0:T(8,128)} %bitcast.16, ...), custom_call_target="tpu_custom_call" | custom-call | tf_op jit(solution)/shard_map/pallas_call | solution.py:609
  121.5 1.5 %copy.19 = bf16[3,1,7168]{2,0,1:T(4,128)(2,1)} copy(bf16[3,1,7168]{2,0,1:T(4,128)(2,1)} %bitcast.14) | data formatting | bytes 86016
  (2 shorter events, 0.0 us)

commit v6 on v5

--- a/solution.py
+++ b/solution.py
@@ -154,7 +154,7 @@
 
 
 def kernel(
-    q_ref, cache_ref, vup_ref, wout_ref, resid_ref, gain_ref, routes_ref, weight_ref,
+    lower_ref, upper_ref, cache_ref, vup_ref, wout_ref, resid_ref, gain_ref, routes_ref, weight_ref,
     wg_ref, wu_ref, wd_ref, out_ref,
     qbuf, kv, score_a, score_b, prob_a, prob_b, oscr, msg, rx1, rx2, rx3, fin, rxz, lat,
     vup, wout, wg, wu, wd, own_resid, heads, pbuf, rxa, ebuf, rxb, zbuf, hid, hidf,
@@ -179,7 +179,8 @@
     mates = [None] + [(gs_of[d], c) for d in (1, 2, 3)]
     far_mates = [(gs_of[d], (x * 4 + y) * 2 + (1 - z)) for d in range(4)]
     columns = pl.ds(pl.multiple_of(g * QUARTER, 128), QUARTER)
-    pairs = [(q_ref, qbuf.at[:, x, y, z])]
+    q_refs = [(lower_ref, upper_ref)[t % 2].at[t // 2] for t in range(6)]
+    pairs = [(q_refs[t], qbuf.at[t, x, y, z]) for t in range(6)]
     pairs += [(cache_ref.at[s], kv.at[s]) for s in range(SEQS)]
     pairs += [
         (vup_ref.at[g], vup),
@@ -204,8 +205,7 @@
     other = 1 - z
 
     def gather_0(k, _):
-        span = pl.ds(*chunks[k])
-        return [wire.push((q_ref, span), (qbuf, span, x, y, z), partner)]
+        return [wire.push((q_refs[k],), (qbuf, k, x, y, z), partner)]
 
     def gather_1(k, copies):
         arrive(copies)
@@ -344,8 +344,10 @@
                     merge([msg[t, part, fs[0], es[0]]] + [rx3[t, part, d] for d in range(3)]),
                 )
 
-        done = [t // 2 for t in range(chunks[k][0], sum(chunks[k])) if t % 2]
-        return [(s, wire.push((fin, 2 * s + other), (rxz, s), partner)) for s in done]
+        finished.add(k)
+        if {2 * (k // 2), 2 * (k // 2) + 1} <= finished:
+            return [(k // 2, wire.push((fin, 2 * (k // 2) + other), (rxz, k // 2), partner))]
+        return []
 
     def reduce_5(k, copies):
         for s, copy in copies:
@@ -353,54 +355,55 @@
             out, peak, total = merge([fin[2 * s + z], rxz[s]])
             lat[s * QROWS : (s + 1) * QROWS, :] = (out / total).astype(BF16)
 
-    state = [None] * len(chunks)
+    state, finished = [None] * len(chunks), set()
 
     def run(steps):
         for step, k in steps:
             state[k] = step(k, state[k])
 
-    loads[0].wait()
-    run([(gather_0, 0), (gather_0, 1)])
-    run([(gather_1, 0), (gather_0, 2), (gather_1, 1)])
-    run([(gather_3, 0), (gather_0, 3), (gather_1, 2)])
-    run([(gather_3, 1), (gather_0, 4), (gather_1, 3)])
-    run([(gather_4, 0), (gather_0, 5), (gather_3, 2)])
-    run([(gather_1, 4), (gather_4, 1), (gather_1, 5)])
+    for copy in loads[:6]:
+        copy.wait()
+    run([(gather_0, 0), (gather_0, 1), (gather_0, 2)])
+    run([(gather_1, 0), (gather_1, 1), (gather_1, 2)])
+    run([(gather_3, 0), (gather_3, 1), (gather_0, 3)])
+    run([(gather_3, 2), (gather_0, 4), (gather_1, 3)])
+    run([(gather_4, 0), (gather_0, 5), (gather_1, 4)])
+    run([(gather_4, 1), (gather_1, 5), (gather_4, 2)])
     run([(gather_3, 3)])
-    for copy in loads[1:4]:
+    for copy in loads[6:9]:
         copy.wait()
     run([(gather_5, 0)])
     between = {
         1: [
-            (gather_4, 2),
             (reduce_1, 0),
+            (gather_3, 5),
+            (gather_5, 2),
             (gather_5, 1),
             (gather_3, 4),
         ],
         2: [
             (gather_4, 3),
-            (gather_5, 2),
-            (gather_3, 5),
             (reduce_1, 1),
+            (reduce_2, 0),
         ],
         3: [
+            (gather_4, 5),
+            (gather_5, 3),
             (reduce_1, 2),
             (gather_4, 4),
-            (reduce_2, 0),
-            (gather_5, 3),
         ],
         4: [
+            (reduce_1, 3),
             (reduce_2, 1),
-            (gather_4, 5),
-            (reduce_1, 3),
+            (gather_5, 5),
+            (reduce_3, 0),
             (reduce_2, 2),
-            (gather_5, 4),
         ],
         5: [
-            (reduce_3, 0),
+            (reduce_1, 5),
+            (reduce_2, 3),
             (reduce_3, 1),
-            (gather_5, 5),
-            (reduce_1, 4),
+            (gather_5, 4),
         ],
     }
 
@@ -413,17 +416,17 @@
                 def _():
                     run(steps)
 
-        attend(t)
-
-    run([(reduce_1, 5), (reduce_4, 0), (reduce_3, 2)])
-    run([(reduce_4, 1), (reduce_2, 3), (reduce_2, 4)])
-    run([(reduce_5, 0), (reduce_2, 5), (reduce_5, 1)])
-    run([(reduce_4, 2), (reduce_3, 3), (reduce_5, 2)])
-    run([(reduce_3, 4), (reduce_3, 5), (reduce_4, 3)])
-    run([(reduce_4, 4), (reduce_4, 5), (reduce_5, 3)])
-    run([(reduce_5, 4), (reduce_5, 5)])
-
-    loads[4].wait()
+        attend(jnp.where(t >= 4, 9 - t, t))
+
+    run([(reduce_1, 4), (reduce_2, 5), (reduce_4, 0)])
+    run([(reduce_3, 2), (reduce_3, 3), (reduce_4, 1)])
+    run([(reduce_2, 4), (reduce_5, 0), (reduce_3, 5)])
+    run([(reduce_5, 1), (reduce_4, 2), (reduce_4, 3)])
+    run([(reduce_3, 4), (reduce_5, 2), (reduce_4, 5)])
+    run([(reduce_5, 3), (reduce_4, 4), (reduce_5, 5)])
+    run([(reduce_5, 4)])
+
+    loads[9].wait()
     heads[g] = mm(lat[...], vup[...]).astype(BF16)
     copies = [wire.push((heads, g), (heads, g), mates[d]) for d in (1, 2, 3)]
     spread, gathered = [], []
@@ -439,7 +442,7 @@
             ((seq < SEQS) & (j == seq * QROWS + row)).astype(F32).astype(BF16)
         )
     arrive(copies)
-    loads[5].wait()
+    loads[10].wait()
     own_resid[...] = jnp.zeros((16, QUARTER), BF16)
     own_resid[0:SEQS, :] = resid_ref[0, :, columns]
     lane = iota((1, 128), 1)
@@ -504,8 +507,8 @@
             copies.append(wire.push(ref, ref, to_f[d]))
     arrive(copies)
 
-    loads[6].wait()
-    loads[7].wait()
+    loads[11].wait()
+    loads[12].wait()
     eye = iota((96, 128), 0) == iota((96, 128), 1)
     squares = jnp.zeros((96, 1), F32)
     gate = jnp.zeros((96, 512), F32)
@@ -554,7 +557,7 @@
     units[g] = (gate / (1.0 + jnp.exp(-gate)) * rise).astype(BF16)
     copies = [wire.push((units, g), (units, g), mates[d]) for d in (1, 2, 3)]
     arrive(copies)
-    loads[8].wait()
+    loads[13].wait()
     for part in range(2):
         cols = pl.ds(part * HALF, HALF)
         value = jnp.zeros((128, HALF), F32)
@@ -605,11 +608,10 @@
     by_column = queries.reshape(SEQS, 16, 8, QK)
     lower = lax.dynamic_index_in_dim(by_column, 2 * pair + core, 2, keepdims=False)
     upper = lax.dynamic_index_in_dim(by_column, 4 + 2 * (1 - pair) + core, 2, keepdims=False)
-    rows = jnp.stack([lower, upper], axis=1).reshape(2 * SEQS, 16, QK)
     mixed = pl.pallas_call(
         kernel,
         out_shape=jax.ShapeDtypeStruct((SEQS, D), BF16),
-        in_specs=[vmem(), hbm(), hbm(), hbm(), vmem(), vmem(), vmem(), vmem(), hbm(), hbm(), hbm()],
+        in_specs=[vmem(), vmem(), hbm(), hbm(), hbm(), vmem(), vmem(), vmem(), vmem(), hbm(), hbm(), hbm()],
         out_specs=vmem(),
         scratch_shapes=[
             pltpu.VMEM((6, 4, 4, 2, 16, QK), BF16),
@@ -654,13 +656,14 @@
             pltpu.VMEM((2, 4, 8, HALF), F32),
             pltpu.SemaphoreType.DMA((250,)),
             pltpu.SemaphoreType.DMA((250,)),
-            pltpu.SemaphoreType.DMA((11,)),
+            pltpu.SemaphoreType.DMA((14,)),
         ],
         compiler_params=pltpu.CompilerParams(
-            collective_id=0, has_side_effects=True, vmem_limit_bytes=60 * 1024 * 1024
+            collective_id=0, has_side_effects=True, vmem_limit_bytes=52 * 1024 * 1024
         ),
     )(
-        rows,
+        lower,
+        upper,
         jnp.swapaxes(cache, 1, 2),
         value_up_weight,
         w_out,

time: 123 us -> 122 us (level)
  local copies, waits for them, and re-layouts: 4.02 us -> 2.63 us
where the time goes in v6:
time: 122 us
  Pallas kernels  119 us (98%)
  local copies, waits for them, and re-layouts  2.63 us (2%)
    pallas_call x1, Pallas kernels, on_device(): pl.pallas_call(kernel, out_shape=jax.ShapeDtypeStruct((SEQS, D), BF16), i...  119 us

profile of v6, /device:TPU:1, one launch (start us, length us, event | category | flops | bytes accessed | tf_op | source)
XLA Modules:
  0.0 121.9 jit_solution(10770616179413492327)
XLA Ops:
  0.0 0.0 copy-start.4
  0.0 0.0 copy-start.3
  0.0 0.0 copy-start.2
  0.0 0.0 copy-start.1
  0.0 0.0 copy-start
  0.1 1.7 %reshape.9 = bf16[3,16,8,576]{3,2,1,0:T(8,128)(2,1)S(1)} reshape(bf16[3,1,73728]{2,0,1:T(4,128)(2,1)} %param.11) | data formatting | bytes 884736 | tf_op jit(solution)/shard_map/reshape | solution.py:608
  1.8 0.3 constant_dynamic-slice_fusion
  2.1 0.0 copy-done.4
  2.1 0.0 copy-done.3
  2.1 0.0 copy-done.2
  2.1 0.0 copy-done.1
  2.1 0.0 copy-done
  2.1 119.2 %shard_map.109 = bf16[3,7168]{1,0:T(4,128)(2,1)S(1)} custom-call(bf16[3,16,576]{2,1,0:T(8,128)(2,1)S(1)} %get-tuple-element.8.lower_ref, bf16[3,16,576]{2,1,0:T(8,128)(2,1)S(1)} %get-tuple-element.7.upper_ref, bf16[3,576,2048]{2,1,0:T(8,128)(2,1)} %bitcast.15, bf16[4,512,128]{2,1,0:T(8,128)(2,1)S(1)} %copy-done, bf16[512,7168]{1,0:T(8,128)(2,1)} %wout_ref.1, ...), custom_call_target="tpu_custom_call" | custom-call | tf_op jit(solution)/shard_map/pallas_call | solution.py:611
  121.3 0.6 copy.19
  (1 shorter events, 0.0 us)
Async XLA Ops:
  0.0 2.1 %copy-start.4 = (bf16[3,1,4]{2,0,1:T(4,128)(2,1)S(1)}, bf16[3,1,4]{2,0,1:T(4,128)(2,1)}, u32[]{:S(2)}) copy-start(bf16[3,1,4]{2,0,1:T(4,128)(2,1)} %param.18) | copy-start | bytes 76
  0.0 2.1 %copy-start.3 = (s32[3,1,4]{2,1,0:T(1,128)S(1)}, s32[3,1,4]{2,1,0:T(1,128)}, u32[]{:S(2)}) copy-start(s32[3,1,4]{2,1,0:T(1,128)} %routes_ref.1) | copy-start | bytes 148
  0.0 2.1 %copy-start.2 = (f32[7168]{0:T(1024)S(1)}, f32[7168]{0:T(1024)}, u32[]{:S(2)}) copy-start(f32[7168]{0:T(1024)} %param.16) | copy-start | bytes 86020
  0.0 2.1 %copy-start.1 = (bf16[3,1,7168]{2,0,1:T(4,128)(2,1)S(1)}, bf16[3,1,7168]{2,0,1:T(4,128)(2,1)}, u32[]{:S(2)}) copy-start(bf16[3,1,7168]{2,0,1:T(4,128)(2,1)} %param.15) | copy-start | bytes 129028
  0.0 2.1 %copy-start = (bf16[4,512,128]{2,1,0:T(8,128)(2,1)S(1)}, bf16[4,512,128]{2,1,0:T(8,128)(2,1)}, u32[]{:S(2)}) copy-start(bf16[4,512,128]{2,1,0:T(8,128)(2,1)} %vup_ref.1) | copy-start | bytes 1572868

commit v7 on v6

--- a/solution.py
+++ b/solution.py
@@ -156,7 +156,7 @@
 def kernel(
     lower_ref, upper_ref, cache_ref, vup_ref, wout_ref, resid_ref, gain_ref, routes_ref, weight_ref,
     wg_ref, wu_ref, wd_ref, out_ref,
-    qbuf, kv, score_a, score_b, prob_a, prob_b, oscr, msg, rx1, rx2, rx3, fin, rxz, lat,
+    qbuf, kv, score_a, score_b, prob_a, prob_b, oscr, msg, rx1, rx2, rx3, fin, rxz,
     vup, wout, wg, wu, wd, own_resid, heads, pbuf, rxa, ebuf, rxb, zbuf, hid, hidf,
     sq, rxs, gs, rxg, units, part_buf, rxq, ybuf, rxy, wbuf, gone, fo,
     send_sems, recv_sems, local_sems,
@@ -353,57 +353,61 @@
         for s, copy in copies:
             copy.wait_recv()
             out, peak, total = merge([fin[2 * s + z], rxz[s]])
-            lat[s * QROWS : (s + 1) * QROWS, :] = (out / total).astype(BF16)
-
-    state, finished = [None] * len(chunks), set()
+            rows = pl.ds(s * QROWS, QROWS)
+            heads[g, rows] = mm((out / total).astype(BF16), vup[...]).astype(BF16)
+            for d in (1, 2, 3):
+                ref = (heads, g, rows)
+                headed.append(wire.push(ref, ref, mates[d]))
+
+    state, finished, headed = [None] * len(chunks), set(), []
 
     def run(steps):
         for step, k in steps:
             state[k] = step(k, state[k])
 
+    run([(gather_0, 0), (gather_0, 1)])
     for copy in loads[:6]:
         copy.wait()
-    run([(gather_0, 0), (gather_0, 1), (gather_0, 2)])
-    run([(gather_1, 0), (gather_1, 1), (gather_1, 2)])
-    run([(gather_3, 0), (gather_3, 1), (gather_0, 3)])
-    run([(gather_3, 2), (gather_0, 4), (gather_1, 3)])
-    run([(gather_4, 0), (gather_0, 5), (gather_1, 4)])
-    run([(gather_4, 1), (gather_1, 5), (gather_4, 2)])
+    run([(gather_1, 0), (gather_1, 1), (gather_0, 2)])
+    run([(gather_0, 3), (gather_3, 0), (gather_1, 2)])
+    run([(gather_0, 4), (gather_3, 1), (gather_1, 3)])
+    run([(gather_4, 0), (gather_1, 4), (gather_0, 5)])
+    run([(gather_3, 2), (gather_4, 1), (gather_1, 5)])
     run([(gather_3, 3)])
-    for copy in loads[6:9]:
+    for copy in loads[6:10]:
         copy.wait()
     run([(gather_5, 0)])
     between = {
         1: [
+            (gather_4, 2),
+            (gather_3, 4),
             (reduce_1, 0),
-            (gather_3, 5),
-            (gather_5, 2),
             (gather_5, 1),
-            (gather_3, 4),
         ],
         2: [
             (gather_4, 3),
+            (gather_3, 5),
             (reduce_1, 1),
-            (reduce_2, 0),
+            (gather_5, 2),
         ],
         3: [
-            (gather_4, 5),
+            (gather_4, 4),
+            (reduce_1, 2),
+            (reduce_2, 0),
             (gather_5, 3),
-            (reduce_1, 2),
-            (gather_4, 4),
         ],
         4: [
+            (gather_4, 5),
+            (gather_5, 4),
             (reduce_1, 3),
             (reduce_2, 1),
-            (gather_5, 5),
-            (reduce_3, 0),
             (reduce_2, 2),
         ],
         5: [
-            (reduce_1, 5),
+            (gather_5, 5),
+            (reduce_1, 4),
             (reduce_2, 3),
-            (reduce_3, 1),
-            (gather_5, 4),
+            (reduce_3, 0),
         ],
     }
 
@@ -416,19 +420,16 @@
                 def _():
                     run(steps)
 
-        attend(jnp.where(t >= 4, 9 - t, t))
-
-    run([(reduce_1, 4), (reduce_2, 5), (reduce_4, 0)])
-    run([(reduce_3, 2), (reduce_3, 3), (reduce_4, 1)])
-    run([(reduce_2, 4), (reduce_5, 0), (reduce_3, 5)])
-    run([(reduce_5, 1), (reduce_4, 2), (reduce_4, 3)])
-    run([(reduce_3, 4), (reduce_5, 2), (reduce_4, 5)])
-    run([(reduce_5, 3), (reduce_4, 4), (reduce_5, 5)])
-    run([(reduce_5, 4)])
-
-    loads[9].wait()
-    heads[g] = mm(lat[...], vup[...]).astype(BF16)
-    copies = [wire.push((heads, g), (heads, g), mates[d]) for d in (1, 2, 3)]
+        attend(t)
+
+    run([(reduce_1, 5), (reduce_3, 2), (reduce_2, 4)])
+    run([(reduce_3, 1), (reduce_3, 3), (reduce_4, 0)])
+    run([(reduce_2, 5), (reduce_4, 2), (reduce_5, 0)])
+    run([(reduce_3, 4), (reduce_4, 1), (reduce_5, 2)])
+    run([(reduce_4, 3), (reduce_3, 5), (reduce_5, 1)])
+    run([(reduce_4, 4), (reduce_5, 3), (reduce_4, 5)])
+    run([(reduce_5, 4), (reduce_5, 5)])
+
     spread, gathered = [], []
     for part in range(2):
         seq, row = padded_row((128, 96), 0, part)
@@ -441,7 +442,7 @@
         gathered.append(
             ((seq < SEQS) & (j == seq * QROWS + row)).astype(F32).astype(BF16)
         )
-    arrive(copies)
+    arrive(headed)
     loads[10].wait()
     own_resid[...] = jnp.zeros((16, QUARTER), BF16)
     own_resid[0:SEQS, :] = resid_ref[0, :, columns]
@@ -627,7 +628,6 @@
             pltpu.VMEM((6, 2, 3, 16, QPAD), BF16),
             pltpu.VMEM((6, 2, 16, QPAD), BF16),
             pltpu.VMEM((SEQS, 2, 16, QPAD), BF16),
-            pltpu.VMEM((96, KVL), BF16),
             pltpu.VMEM((KVL, DV), BF16),
             pltpu.VMEM((512, QUARTER), BF16),
             pltpu.VMEM((QUARTER, 512), BF16),

time: 122 us -> 120 us (0.984)
  Pallas kernels: 119 us -> 117 us
    pallas_call x1, Pallas kernels: 119 us -> 117 us  [on_device(): pl.pallas_call(kernel, out_shape=jax.ShapeDtypeStruct((SEQS, D), BF16), i...]
where the time goes in v7:
time: 120 us
  Pallas kernels  117 us (98%)
  local copies, waits for them, and re-layouts  2.63 us (2%)
    pallas_call x1, Pallas kernels, on_device(): pl.pallas_call(kernel, out_shape=jax.ShapeDtypeStruct((SEQS, D), BF16), i...  117 us

profile of v7, /device:TPU:1, one launch (start us, length us, event | category | flops | bytes accessed | tf_op | source)
XLA Modules:
  0.0 119.9 jit_solution(11586400463859337373)
XLA Ops:
  0.0 0.0 copy-start.4
  0.0 0.0 copy-start.3
  0.0 0.0 copy-start.2
  0.0 0.0 copy-start.1
  0.0 0.0 copy-start
  0.1 1.7 %reshape.9 = bf16[3,16,8,576]{3,2,1,0:T(8,128)(2,1)S(1)} reshape(bf16[3,1,73728]{2,0,1:T(4,128)(2,1)} %param.11) | data formatting | bytes 884736 | tf_op jit(solution)/shard_map/reshape | solution.py:609
  1.8 0.3 constant_dynamic-slice_fusion
  2.1 0.0 copy-done.4
  2.1 0.0 copy-done.3
  2.1 0.0 copy-done.2
  2.1 0.0 copy-done.1
  2.1 0.0 copy-done
  2.1 117.1 %shard_map.109 = bf16[3,7168]{1,0:T(4,128)(2,1)S(1)} custom-call(bf16[3,16,576]{2,1,0:T(8,128)(2,1)S(1)} %get-tuple-element.8.lower_ref, bf16[3,16,576]{2,1,0:T(8,128)(2,1)S(1)} %get-tuple-element.7.upper_ref, bf16[3,576,2048]{2,1,0:T(8,128)(2,1)} %bitcast.15, bf16[4,512,128]{2,1,0:T(8,128)(2,1)S(1)} %copy-done, bf16[512,7168]{1,0:T(8,128)(2,1)} %wout_ref.1, ...), custom_call_target="tpu_custom_call" | custom-call | tf_op jit(solution)/shard_map/pallas_call | solution.py:612
  119.3 0.6 copy.19
  (1 shorter events, 0.0 us)
Async XLA Ops:
  0.0 2.1 %copy-start.4 = (bf16[3,1,4]{2,0,1:T(4,128)(2,1)S(1)}, bf16[3,1,4]{2,0,1:T(4,128)(2,1)}, u32[]{:S(2)}) copy-start(bf16[3,1,4]{2,0,1:T(4,128)(2,1)} %param.18) | copy-start | bytes 76
  0.0 2.1 %copy-start.3 = (s32[3,1,4]{2,1,0:T(1,128)S(1)}, s32[3,1,4]{2,1,0:T(1,128)}, u32[]{:S(2)}) copy-start(s32[3,1,4]{2,1,0:T(1,128)} %routes_ref.1) | copy-start | bytes 148
  0.0 2.1 %copy-start.2 = (f32[7168]{0:T(1024)S(1)}, f32[7168]{0:T(1024)}, u32[]{:S(2)}) copy-start(f32[7168]{0:T(1024)} %param.16) | copy-start | bytes 86020
  0.0 2.1 %copy-start.1 = (bf16[3,1,7168]{2,0,1:T(4,128)(2,1)S(1)}, bf16[3,1,7168]{2,0,1:T(4,128)(2,1)}, u32[]{:S(2)}) copy-start(bf16[3,1,7168]{2,0,1:T(4,128)(2,1)} %param.15) | copy-start | bytes 129028
  0.0 2.1 %copy-start = (bf16[4,512,128]{2,1,0:T(8,128)(2,1)S(1)}, bf16[4,512,128]{2,1,0:T(8,128)(2,1)}, u32[]{:S(2)}) copy-start(bf16[4,512,128]{2,1,0:T(8,128)(2,1)} %vup_ref.1) | copy-start | bytes 1572868

commit v8 on v7

--- a/solution.py
+++ b/solution.py
@@ -446,6 +446,19 @@
     loads[10].wait()
     own_resid[...] = jnp.zeros((16, QUARTER), BF16)
     own_resid[0:SEQS, :] = resid_ref[0, :, columns]
+    def scatter(source, landing, part):
+        fs, es, to_f, to_e = axes[part]
+        return [
+            wire.push((source, part, fs[d]), (landing, part, d - 1), to_f[d]) for d in (1, 2, 3)
+        ]
+
+    def summed(first, landing, part):
+        value = first.astype(F32)
+        for d in range(3):
+            value = value + landing[part, d].astype(F32)
+        return value
+
+    copies = []
     lane = iota((1, 128), 1)
     gates = jnp.zeros((1, 128), F32)
     for s in range(SEQS):
@@ -465,48 +478,34 @@
             seq, row = padded_row((128, 128), 0, part)
             head = jnp.where((seq == SEQS) & (row == c), gates, value[:, :128])
             pbuf[part, :, :, :128] = head.astype(BF16).reshape(4, 32, 128)
-
-    def scatter(source, landing):
-        copies = []
-        for part, (fs, es, to_f, to_e) in enumerate(axes):
-            for d in (1, 2, 3):
-                copies.append(wire.push((source, part, fs[d]), (landing, part, d - 1), to_f[d]))
-        return copies
-
-    def summed(first, landing, part):
-        value = first.astype(F32)
-        for d in range(3):
-            value = value + landing[part, d].astype(F32)
-        return value
-
-    copies = scatter(pbuf, rxa)
-    arrive(copies)
-    copies = []
+        copies.append(scatter(pbuf, rxa, part))
+
+    before, copies = copies, []
     for part, (fs, es, to_f, to_e) in enumerate(axes):
+        arrive(before[part])
         value = summed(pbuf[part, fs[0]], rxa, part)
         for k in range(4):
             ebuf[part, k] = fold(value[k * 8 : (k + 1) * 8])
-        for d in (1, 2, 3):
-            copies.append(wire.push((ebuf, part, es[d]), (rxb, part, d - 1), to_e[d]))
-    arrive(copies)
-    copies = []
+        copies.append(
+            [wire.push((ebuf, part, es[d]), (rxb, part, d - 1), to_e[d]) for d in (1, 2, 3)]
+        )
+    before, copies = copies, []
     for part, (fs, es, to_f, to_e) in enumerate(axes):
+        arrive(before[part])
         zbuf[part, z, es[0]] = summed(ebuf[part, es[0]], rxb, part).astype(BF16)
         ref = (zbuf, part, z, es[0])
-        for peer in [far] + to_e[1:] + far_e[part][1:]:
-            copies.append(wire.push(ref, ref, peer))
-    arrive(copies)
-    copies = []
+        peers = [far] + to_e[1:] + far_e[part][1:]
+        copies.append([wire.push(ref, ref, peer) for peer in peers])
+    before, copies = copies, []
     for part, (fs, es, to_f, to_e) in enumerate(axes):
+        arrive(before[part])
         for k in range(4):
             hidf[part, k] = (
                 (unfold(zbuf[part, 0, k]) + unfold(zbuf[part, 1, k])).astype(BF16).astype(F32)
             )
         hid[part, fs[0]] = hidf[part].reshape(32, HALF).astype(BF16)
-        for d in (1, 2, 3):
-            ref = (hid, part, fs[0])
-            copies.append(wire.push(ref, ref, to_f[d]))
-    arrive(copies)
+        ref = (hid, part, fs[0])
+        copies.append([wire.push(ref, ref, to_f[d]) for d in (1, 2, 3)])
 
     loads[11].wait()
     loads[12].wait()
@@ -515,6 +514,7 @@
     gate = jnp.zeros((96, 512), F32)
     rise = jnp.zeros((96, 512), F32)
     for part in range(2):
+        arrive(copies[part])
         rows = mm(gathered[part], hid[part].reshape(128, HALF))
         squares = squares + jnp.sum(rows * rows, axis=-1, keepdims=True)
         cols = pl.ds(part * HALF, HALF)
@@ -558,6 +558,7 @@
     units[g] = (gate / (1.0 + jnp.exp(-gate)) * rise).astype(BF16)
     copies = [wire.push((units, g), (units, g), mates[d]) for d in (1, 2, 3)]
     arrive(copies)
+    before = []
     loads[13].wait()
     for part in range(2):
         cols = pl.ds(part * HALF, HALF)
@@ -567,15 +568,16 @@
             value = value + mm(rows, wd[k * 128 : (k + 1) * 128, cols])
         value = value.astype(BF16).astype(F32) * factors[part]
         part_buf[part] = value.astype(BF16).reshape(4, 32, HALF)
-    copies = scatter(part_buf, rxq)
-    arrive(copies)
+        before.append(scatter(part_buf, rxq, part))
     copies = []
     for part, (fs, es, to_f, to_e) in enumerate(axes):
+        arrive(before[part])
         ybuf[part] = summed(part_buf[part, fs[0]], rxq, part).reshape(4, 8, HALF)
-        for d in (1, 2, 3):
-            copies.append(wire.push((ybuf, part, es[d]), (rxy, part, d - 1), to_e[d]))
-    arrive(copies)
+        copies.append(
+            [wire.push((ybuf, part, es[d]), (rxy, part, d - 1), to_e[d]) for d in (1, 2, 3)]
+        )
     for part, (fs, es, to_f, to_e) in enumerate(axes):
+        arrive(copies[part])
         wbuf[part] = summed(ybuf[part, es[0]], rxy, part)
     for part, (fs, es, to_f, to_e) in enumerate(axes):
         value, whole = wbuf[part], hidf[part, es[0]] + wbuf[part]

time: 120 us -> 121 us (level)
  no operation moved by 1% of the time
where the time goes in v8:
time: 121 us; the launch traced here: 120 us
  Pallas kernels  118 us (98%)
  local copies, waits for them, and re-layouts  2.63 us (2%)
    pallas_call x1, Pallas kernels, on_device(): pl.pallas_call(kernel, out_shape=jax.ShapeDtypeStruct((SEQS, D), BF16), i...  118 us

profile of v8, /device:TPU:1, one launch (start us, length us, event | category | flops | bytes accessed | tf_op | source)
XLA Modules:
  0.0 120.4 jit_solution(3779644181415528278)
XLA Ops:
  0.0 0.0 copy-start.4
  0.0 0.0 copy-start.3
  0.0 0.0 copy-start.2
  0.0 0.0 copy-start.1
  0.0 0.0 copy-start
  0.1 1.7 %reshape.9 = bf16[3,16,8,576]{3,2,1,0:T(8,128)(2,1)S(1)} reshape(bf16[3,1,73728]{2,0,1:T(4,128)(2,1)} %param.11) | data formatting | bytes 884736 | tf_op jit(solution)/shard_map/reshape | solution.py:611
  1.8 0.3 constant_dynamic-slice_fusion
  2.1 0.0 copy-done.4
  2.1 0.0 copy-done.3
  2.1 0.0 copy-done.2
  2.1 0.0 copy-done.1
  2.1 0.0 copy-done
  2.1 117.7 %shard_map.109 = bf16[3,7168]{1,0:T(4,128)(2,1)S(1)} custom-call(bf16[3,16,576]{2,1,0:T(8,128)(2,1)S(1)} %get-tuple-element.8.lower_ref, bf16[3,16,576]{2,1,0:T(8,128)(2,1)S(1)} %get-tuple-element.7.upper_ref, bf16[3,576,2048]{2,1,0:T(8,128)(2,1)} %bitcast.15, bf16[4,512,128]{2,1,0:T(8,128)(2,1)S(1)} %copy-done, bf16[512,7168]{1,0:T(8,128)(2,1)} %wout_ref.1, ...), custom_call_target="tpu_custom_call" | custom-call | tf_op jit(solution)/shard_map/pallas_call | solution.py:614
  119.8 0.6 copy.19
  (1 shorter events, 0.0 us)
Async XLA Ops:
  0.0 2.1 %copy-start.4 = (bf16[3,1,4]{2,0,1:T(4,128)(2,1)S(1)}, bf16[3,1,4]{2,0,1:T(4,128)(2,1)}, u32[]{:S(2)}) copy-start(bf16[3,1,4]{2,0,1:T(4,128)(2,1)} %param.18) | copy-start | bytes 76
  0.0 2.1 %copy-start.3 = (s32[3,1,4]{2,1,0:T(1,128)S(1)}, s32[3,1,4]{2,1,0:T(1,128)}, u32[]{:S(2)}) copy-start(s32[3,1,4]{2,1,0:T(1,128)} %routes_ref.1) | copy-start | bytes 148
  0.0 2.1 %copy-start.2 = (f32[7168]{0:T(1024)S(1)}, f32[7168]{0:T(1024)}, u32[]{:S(2)}) copy-start(f32[7168]{0:T(1024)} %param.16) | copy-start | bytes 86020
  0.0 2.1 %copy-start.1 = (bf16[3,1,7168]{2,0,1:T(4,128)(2,1)S(1)}, bf16[3,1,7168]{2,0,1:T(4,128)(2,1)}, u32[]{:S(2)}) copy-start(bf16[3,1,7168]{2,0,1:T(4,128)(2,1)} %param.15) | copy-start | bytes 129028
  0.0 2.1 %copy-start = (bf16[4,512,128]{2,1,0:T(8,128)(2,1)S(1)}, bf16[4,512,128]{2,1,0:T(8,128)(2,1)}, u32[]{:S(2)}) copy-start(bf16[4,512,128]{2,1,0:T(8,128)(2,1)} %vup_ref.1) | copy-start | bytes 1572868
